TPU v7x, 128 devices: a whole 4x4x4 slice. The times are simulated.
128 devices in a mesh: src: 8 (over y, x_lo), tgt: 16 (over z, x_hi, core).
Axes of the slice: x: 4 (x_hi: 2, x_lo: 2; x = x_hi * 2 + x_lo), y: 4, z: 4, core: 2. Of those that a mesh axis runs over, the one named last changes fastest.
Arguments:
- coeffs: bfloat16 [8, 16, 16, 128, 256], P('src', 'tgt'), may hold values from -6 to 6
- weights: bfloat16 [8, 16, 16, 11, 64, 256], P('src', 'tgt'), may hold values from -0.375 to 0.375
- evaluate: bfloat16 [16, 16, 8, 1024, 128], P('tgt', 'src'), may hold values from -0.1875 to 0.1875
Outputs:
- field_image: bfloat16 [16, 16, 1024, 256], P('tgt', 'src')
All inputs are finite; a program needn't handle non-finite values.
Results may differ from a plain program's by a relative error of at most 0.024.
Values may be sent and summed in bfloat16 or wider, within the bound.
No kernel may reach another device: no remote copies, remote signals or barrier semaphores. Data moves between devices by JAX's collectives and lax.ppermute only.
A program may use at most 64 MiB of HBM per device.

v0:
```python
import jax
import jax.numpy as jnp
from jax import lax
from jax.experimental import pallas as pl
from jax.experimental.pallas import tpu as pltpu
from jax.sharding import PartitionSpec as P

BF16 = jnp.bfloat16
LIMIT = 40 * 1024 * 1024
LOCAL = 4


def stacked(w):
    n = w.shape[0]
    parts = [w[:, i * n : (i + 1) * n] for i in range(4)]
    top = jnp.concatenate([parts[0], -parts[1], parts[2], -parts[3]], axis=1)
    low = jnp.concatenate([parts[1], parts[0], parts[3], parts[2]], axis=1)
    return jnp.concatenate([top, low], axis=0)


def combine(w, own, partner):
    both = jnp.concatenate([own, partner], axis=0)
    return jnp.dot(stacked(w), both, preferred_element_type=jnp.float32).astype(BF16)


def combine_pair(wa, wb, xa, xb):
    n = 2 * wa.shape[0]
    first, second = stacked(wa), stacked(wb)
    second = jnp.concatenate([second[:, n:], second[:, :n]], axis=1)
    lhs = jnp.concatenate([first, second], axis=0)
    out = jnp.dot(lhs, jnp.concatenate([xa, xb], axis=0), preferred_element_type=jnp.float32)
    out = out.astype(BF16)
    return out[:n], out[n:]


def call(body, out_shapes, args, specs=None, scratch=(), flops=0, moved=0):
    return pl.pallas_call(
        body,
        out_shape=[jax.ShapeDtypeStruct(s, BF16) for s in out_shapes],
        in_specs=specs or [pl.BlockSpec(memory_space=pltpu.VMEM)] * len(args),
        out_specs=[pl.BlockSpec(memory_space=pltpu.VMEM)] * len(out_shapes),
        scratch_shapes=list(scratch),
        cost_estimate=pl.CostEstimate(flops=0, bytes_accessed=1, transcendentals=0),
        compiler_params=pltpu.CompilerParams(vmem_limit_bytes=LIMIT),
    )(*args)


class Order:
    def __init__(self):
        self.last = None

    def level(self, arrays, weights, outs, paired=False, after=()):
        na, nw = len(arrays), len(weights)
        rows, shots = arrays[0].shape[1:]

        def body(*refs):
            x, w, o = refs[:na], refs[na : na + nw], refs[len(args) :]
            flip = lax.axis_index("src") * 2

            def get(refs, at):
                if len(at) == 2:
                    return refs[at[0]][at[1]]
                return refs[at[0]][jnp.bitwise_xor(at[1], flip), at[2]]

            for k, jobs in enumerate(outs):
                if paired:
                    for i in range(0, len(jobs), 2):
                        (xa, xb, wa), (_, _, wb) = jobs[i], jobs[i + 1]
                        o[k][i], o[k][i + 1] = combine_pair(get(w, wa), get(w, wb), get(x, xa), get(x, xb))
                else:
                    for i, (xa, xb, wa) in enumerate(jobs):
                        o[k][i] = combine(get(w, wa), get(x, xa), get(x, xb))

        args = list(arrays) + list(weights) + list(after)
        if self.last is not None:
            args.append(self.last)
        jobs = sum(len(j) for j in outs)
        results = call(
            body,
            [(len(j), rows, shots) for j in outs],
            args,
            flops=2 * jobs * rows * 2 * rows * shots,
            moved=jobs * rows * shots * 4,
        )
        self.last = results[0]
        return results

    def split(self, weights, plan, boxes):
        rank, cols = weights.shape[2:]

        def body(w, _, *refs):
            outs, sems = refs[:-1], refs[-1]
            flip = lax.axis_index("src") * 2
            copies = []
            for i, ((b0, b1, b2, b3), first, k, at) in enumerate(plan):
                box = jnp.bitwise_xor(b0 + 2 * b1 + 4 * b2 + 8 * b3, flip)
                copies.append(pltpu.make_async_copy(w.at[box, pl.ds(first, 2)], outs[k].at[at], sems.at[i]))
            for c in copies:
                c.start()
            for c in copies:
                c.wait()

        results = call(
            body,
            [(n, 2, rank, cols) for n in boxes],
            [weights, self.last],
            specs=[pl.BlockSpec(memory_space=pltpu.HBM), pl.BlockSpec(memory_space=pltpu.VMEM)],
            scratch=[pltpu.SemaphoreType.DMA((len(plan),))],
            moved=1,
        )
        self.last = results[0]
        return results

    def local_levels(self, coeffs, weights):
        loc, rows, shots = coeffs.shape
        rank, cols = weights.shape[2:]

        def body(x_hbm, w, out0, out1, early, x, wbuf, buf, sem, sems, early_sem):
            flip = lax.axis_index("src") * 2

            def actual(r):
                b0, b1, b2, b3 = r >> 3, (r >> 2) & 1, (r >> 1) & 1, r & 1
                return jnp.bitwise_xor(b0 + 2 * b1 + 4 * b2 + 8 * b3, flip)

            fetch = pltpu.make_async_copy(x_hbm, x, sem)
            fetch.start()
            copies = [
                pltpu.make_async_copy(w.at[:, l], wbuf.at[l], sems.at[l]) for l in range(LOCAL)
            ]
            copies[0].start()
            later = [pltpu.make_async_copy(w.at[:, pl.ds(LOCAL, 3)], early, early_sem)]
            fetch.wait()
            for l in range(LOCAL):
                copies[l].wait()
                if l == 0:
                    for c in copies[1:] + later:
                        c.start()
                src = x if l == 0 else buf.at[(l - 1) % 2]
                dst = buf.at[l % 2]
                if l < LOCAL - 1:
                    for b in range(loc):
                        far = b ^ (1 << l)
                        if b < far:
                            dst[b], dst[far] = combine_pair(wbuf[l, b], wbuf[l, far], src[b], src[far])
                else:
                    for r in range(0, loc, 2):
                        b, far = actual(r), actual(r + 1)
                        out = out1 if r >= loc // 2 else out0
                        i = r % (loc // 2)
                        out[i], out[i + 1] = combine_pair(wbuf[l, b], wbuf[l, far], src[b], src[far])
            for c in later:
                c.wait()

        results = call(
            body,
            [(loc // 2, rows, shots)] * 2 + [(loc, 3, rank, cols)],
            [coeffs, weights],
            specs=[pl.BlockSpec(memory_space=pltpu.HBM)] * 2,
            scratch=[
                pltpu.VMEM((loc, rows, shots), BF16),
                pltpu.VMEM((LOCAL, loc, rank, cols), BF16),
                pltpu.VMEM((2, loc, rows, shots), BF16),
                pltpu.SemaphoreType.DMA,
                pltpu.SemaphoreType.DMA((LOCAL,)),
                pltpu.SemaphoreType.DMA,
            ],
            flops=2 * LOCAL * loc * rows * 2 * rows * shots,
            moved=LOCAL * loc * rank * cols * 2,
        )
        self.last = results[0]
        return results

    def evaluated(self, evaluate, kept, came, box, field):
        boxes, sources, points, rows = evaluate.shape
        shots = kept.shape[2]
        tile = 256

        def body(e, k, c, _, out, buf, sems):
            me = lax.axis_index("src")
            copies = []
            for i in range(points // tile):
                rng = slice(i * tile, (i + 1) * tile)
                total = jnp.zeros((tile, shots), jnp.float32)
                for pair in range(sources // 2):
                    b2, b1 = pair >> 1, pair & 1
                    near = jnp.bitwise_xor(me, 2 * b1 + 4 * b2)
                    far = jnp.bitwise_xor(near, 1)
                    lhs = jnp.concatenate([e[box, near, rng], e[box, far, rng]], axis=1)
                    rhs = jnp.concatenate([k[pair], c[pair]], axis=0)
                    total += jnp.dot(lhs, rhs, preferred_element_type=jnp.float32)
                buf[i] = total.astype(BF16)
                copies.append(pltpu.make_async_copy(buf.at[i], out.at[box, pl.ds(i * tile, tile)], sems.at[i]))
                copies[-1].start()
            for copy in copies:
                copy.wait()

        vmem = pl.BlockSpec(memory_space=pltpu.VMEM)
        hbm = pl.BlockSpec(memory_space=pltpu.HBM)
        out = pl.pallas_call(
            body,
            out_shape=jax.ShapeDtypeStruct((boxes, points, shots), BF16),
            in_specs=[vmem, vmem, vmem, vmem if field is None else hbm],
            out_specs=hbm,
            input_output_aliases={} if field is None else {3: 0},
            scratch_shapes=[
                pltpu.VMEM((points // tile, tile, shots), BF16),
                pltpu.SemaphoreType.DMA((points // tile,)),
            ],
            cost_estimate=pl.CostEstimate(
                flops=2 * sources * points * rows * shots,
                bytes_accessed=2 * sources * points * rows + 2 * points * shots,
                transcendentals=0,
            ),
            compiler_params=pltpu.CompilerParams(vmem_limit_bytes=LIMIT),
        )(evaluate, kept, came, self.last if field is None else field)
        return out


def swapped(shard, axis, mask):
    return lax.ppermute(shard, axis, [(i, i ^ mask) for i in range(lax.axis_size(axis))])


def shards(coeffs, weights, evaluate):
    coeffs, weights, evaluate = coeffs[0, 0], weights[0, 0], evaluate[0]
    coeffs = pltpu.with_memory_space_constraint(coeffs, pltpu.HBM)
    weights = pltpu.with_memory_space_constraint(weights, pltpu.HBM)
    order = Order()
    half0, half1, early = order.local_levels(coeffs, weights)
    halves = (half0, half1)

    def box(b0, b1, b2, b3):
        return b0 + 2 * b1 + 4 * b2 + 8 * b3

    def level4(b0, facing):
        jobs = [((0, i), (1, i), (0, box(b0, i >> 2, (i >> 1) & 1, i & 1), 0)) for i in range(8)]
        return order.level([halves[b0], facing], [early], [jobs])[0]

    def level5(b0, x, far, after):
        jobs = [
            [((0, 4 * b1 + i), (1, 4 * (1 - b1) + i), (0, box(b0, b1, i >> 1, i & 1), 1)) for i in range(4)]
            for b1 in range(2)
        ]
        return order.level([x, far], [early], jobs, after=after)

    def level6(c, x, far, after):
        jobs = [
            [((0, 2 * b2 + b3), (1, 2 * b2 + b3), (0, box(c[0], c[1], b2, b3), 2)) for b3 in range(2)]
            for b2 in range(2)
        ]
        return order.level([x, far], [early], jobs, after=after)

    def level7(c, keep, came, after):
        q = 2 * c[1] + c[0]
        jobs = [((r1, b3), (1 - r1, b3), (r1, (b3 * 4 + q, 0))) for b3 in range(2) for r1 in range(2)]
        return order.level([keep, came], [keep78, got1], [jobs], paired=True, after=after)[0]

    def level8(c, x, far):
        q = 2 * c[1] + c[0]
        jobs = [
            [((0, 2 * b3 + r1), (1, 2 * b3 + r1), (r1, (b3 * 4 + q, 1))) for r1 in range(2)]
            for b3 in range(2)
        ]
        return order.level([x, far], [keep78, got1], jobs)

    def late(c, r2, r1, l):
        q = 2 * c[1] + c[0]
        return ((0, (q, l)), (1, (8 + q, l)), (2, (q, l)), (3, (q, l)))[2 * r2 + r1]

    def level9(c, keep, came, after):
        jobs = [((r2, r1), (1 - r2, r1), late(c, r2, r1, 0)) for r1 in range(2) for r2 in range(2)]
        return order.level([keep, came], [keep9, got1, got2, got3], [jobs], paired=True, after=after)[0]

    def level10(c, x, far):
        jobs = [
            ((0, 2 * r1 + r2), (1, 2 * r1 + r2), late(c, r2, r1, 1)) for r2 in range(2) for r1 in range(2)
        ]
        return order.level([x, far], [keep9, got1, got2, got3], [jobs])[0]

    P0, Q0, P1, Q1 = (0, 1), (0, 0), (1, 1), (1, 0)
    near, far, keep, send, came, spread, fields = {}, {}, {}, {}, {}, {}, []

    facing = [swapped(h, "tgt", 1) for h in halves]

    def do4(b0):
        spread[b0] = level4(b0, facing[b0])
        far[b0] = swapped(spread[b0], "src", 1)

    def do5(b0, after):
        near[b0, 0], near[b0, 1] = level5(b0, spread[b0], far[b0], after)
        for b1 in (1, 0):
            far[b0, b1] = swapped(near[b0, b1], "tgt", 2)

    def do6(c, after=()):
        keep[c], send[c] = level6(c, near[c], far[c], after)
        came[c] = swapped(send[c], "src", 2)

    def do7(c, after=()):
        near[c] = level7(c, keep[c], came[c], after)
        far[c] = swapped(near[c], "tgt", 4)

    def do8(c):
        keep[c], send[c] = level8(c, near[c], far[c])
        came[c] = swapped(send[c], "src", 4)

    def do9(c, after=()):
        near[c] = level9(c, keep[c], came[c], after)
        far[c] = swapped(near[c], "tgt", 8)

    def do10(c):
        near[c] = level10(c, near[c], far[c])
        if c[1]:
            came[c] = swapped(near[c], "src", 1)

    def finish(b0):
        before = fields[-1] if fields else None
        fields.append(order.evaluated(evaluate, near[b0, 0], came[b0, 1], b0, before))

    two, quads = (0, 1), [(q & 1, q >> 1) for q in range(4)]
    plan = [((b0, b1, b2, 1), 9, b2, 2 * b1 + b0) for b0, b1 in quads for b2 in two]
    send2, send3 = order.split(weights, plan, (4, 4))
    do4(0), do4(1)
    plan = [((b0, b1, b2, b3), 7, b2, b3 * 4 + 2 * b1 + b0) for b2 in two for b3 in two for b0, b1 in quads]
    plan += [((b0, b1, 1, 0), 9, 1, 8 + 2 * b1 + b0) for b0, b1 in quads]
    plan += [((b0, b1, 0, 0), 9, 2, 2 * b1 + b0) for b0, b1 in quads]
    keep78, send1, keep9 = order.split(weights, plan, (8, 12, 4))
    got1, got2, got3 = swapped(send1, "src", 2), swapped(send2, "src", 4), swapped(send3, "src", 6)
    do5(0, ()), do5(1, ())
    do6(P0, (got1,)), do7(P0, (got2, got3)), do6(P1), do6(Q0), do7(P1), do8(P0), do7(Q0), do6(Q1)
    do9(P0), do8(P1), do7(Q1), do8(Q0), do9(P1), do9(Q0), do10(P0), do8(Q1)
    do10(P1), do9(Q1), do10(Q0), finish(0), do10(Q1), finish(1)
    field = fields[-1]
    return field[None]


def solution(mesh):
    placed = (
        P("src", "tgt", None, None, None),
        P("src", "tgt", None, None, None, None),
        P("tgt", "src", None, None, None),
    )
    return jax.shard_map(
        shards, mesh=mesh, in_specs=placed, out_specs=P("tgt", "src", None, None), check_vma=False
    )
```

profile of v0, /device:TPU:0, one launch (start us, length us, event | category | flops | bytes accessed | tf_op | source)
XLA Modules:
  0.0 101.2 jit_solution(4387587490960869310)
XLA Ops:
  0.0 4.7 %shard_map.37 = (bf16[8,128,256]{2,1,0:T(8,128)(2,1)S(1)}, bf16[8,128,256]{2,1,0:T(8,128)(2,1)S(1)}, bf16[16,3,64,256]{3,2,1,0:T(8,128)(2,1)S(1)}) custom-call(bf16[16,128,256]{2,1,0:T(8,128)(2,1)} %bitcast.9, bf16[16,11,64,256]{3,2,1,0:T(8,128)(2,1)} %bitcast.6), custom_call_target="tpu_custom_call" | custom-call | bytes 1 | tf_op jit(solution)/shard_map/pallas_call | solution.py:37
  4.8 0.5 collective-permute-start
  5.3 1.1 %shard_map.38 = (bf16[4,2,64,256]{3,2,1,0:T(8,128)(2,1)S(1)}, bf16[4,2,64,256]{3,2,1,0:T(8,128)(2,1)S(1)}) custom-call(bf16[16,11,64,256]{3,2,1,0:T(8,128)(2,1)} %bitcast.7, bf16[8,128,256]{2,1,0:T(8,128)(2,1)S(1)} %get-tuple-element.35._.refs_0_), custom_call_target="tpu_custom_call" | custom-call | bytes 1 | tf_op jit(solution)/shard_map/pallas_call | solution.py:37
  6.7 0.5 shard_map.39.refs_3_.refs_0_
  7.2 1.7 %collective-permute-start.3 = (bf16[8,128,256]{2,1,0:T(8,128)(2,1)S(1)}, bf16[8,128,256]{2,1,0:T(8,128)(2,1)S(1)}, u32[]{:S(2)}, u32[]{:S(2)}) collective-permute-start(bf16[8,128,256]{2,1,0:T(8,128)(2,1)S(1)} %shard_map.39.refs_3_.refs_0_), channel_id=1, source_target_pairs={{0,16},{16,0},{32,48},{48,32},{64,80},{80,64},{96,112},{112,96},{1... | collective-permute-start | bytes 1572872 | tf_op jit(solution)/shard_map/ppermute | solution.py:220
  8.9 0.5 shard_map.40._.refs_0_
  9.4 1.6 %shard_map.41 = (bf16[8,2,64,256]{3,2,1,0:T(8,128)(2,1)S(1)}, bf16[12,2,64,256]{3,2,1,0:T(8,128)(2,1)S(1)}, bf16[4,2,64,256]{3,2,1,0:T(8,128)(2,1)S(1)}) custom-call(bf16[16,11,64,256]{3,2,1,0:T(8,128)(2,1)} %bitcast.8, bf16[8,128,256]{2,1,0:T(8,128)(2,1)S(1)} %shard_map.40._.refs_0_), custom_call_target="tpu_custom_call" | custom-call | bytes 1 | tf_op jit(solution)/shard_map/pallas_call | solution.py:37
  11.0 1.7 %collective-permute-start.8 = (bf16[12,2,64,256]{3,2,1,0:T(8,128)(2,1)S(1)}, bf16[12,2,64,256]{3,2,1,0:T(8,128)(2,1)S(1)}, u32[]{:S(2)}, u32[]{:S(2)}) collective-permute-start(bf16[12,2,64,256]{3,2,1,0:T(8,128)(2,1)S(1)} %get-tuple-element.42), channel_id=1, source_target_pairs={{0,32},{16,48},{32,0},{48,16},{64,96},{80,112},{96,64},{112,80},{1... | collective-permute-start | bytes 2359304 | tf_op jit(solution)/shard_map/ppermute | solution.py:220
  12.7 0.5 collective-permute-start.2
  13.2 8.9 %collective-permute-done.3.refs_1_ = bf16[8,128,256]{2,1,0:T(8,128)(2,1)S(1)} collective-permute-done((bf16[8,128,256]{2,1,0:T(8,128)(2,1)S(1)}, bf16[8,128,256]{2,1,0:T(8,128)(2,1)S(1)}, u32[]{:S(2)}, u32[]{:S(2)}) %collective-permute-start.3) | collective-permute-done | bytes 524320 | tf_op jit(solution)/shard_map/ppermute | solution.py:220
  22.1 0.5 shard_map.42
  22.6 3.2 %collective-permute-start.7 = (bf16[4,128,256]{2,1,0:T(8,128)(2,1)S(1)}, bf16[4,128,256]{2,1,0:T(8,128)(2,1)S(1)}, u32[]{:S(2)}, u32[]{:S(2)}) collective-permute-start(bf16[4,128,256]{2,1,0:T(8,128)(2,1)S(1)} %get-tuple-element.41.refs_0_), channel_id=1, source_target_pairs={{0,2},{1,3},{2,0},{3,1},{4,6},{5,7},{6,4},{7,5},{8,10},{9,11},{10,... | collective-permute-start | bytes 786440 | tf_op jit(solution)/shard_map/ppermute | solution.py:220
  25.8 3.2 %collective-permute-start.10 = (bf16[4,2,64,256]{3,2,1,0:T(8,128)(2,1)S(1)}, bf16[4,2,64,256]{3,2,1,0:T(8,128)(2,1)S(1)}, u32[]{:S(2)}, u32[]{:S(2)}) collective-permute-start(bf16[4,2,64,256]{3,2,1,0:T(8,128)(2,1)S(1)} %get-tuple-element.36.refs_3_), channel_id=1, source_target_pairs={{0,64},{16,80},{32,96},{48,112},{64,0},{80,16},{96,32},{112,48},{1... | collective-permute-start | bytes 786440 | tf_op jit(solution)/shard_map/ppermute | solution.py:220
  29.0 1.0 %collective-permute-start.11 = (bf16[4,2,64,256]{3,2,1,0:T(8,128)(2,1)S(1)}, bf16[4,2,64,256]{3,2,1,0:T(8,128)(2,1)S(1)}, u32[]{:S(2)}, u32[]{:S(2)}) collective-permute-start(bf16[4,2,64,256]{3,2,1,0:T(8,128)(2,1)S(1)} %get-tuple-element.45), channel_id=1, source_target_pairs={{0,96},{16,112},{32,64},{48,80},{64,32},{80,48},{96,0},{112,16},{1... | collective-permute-start | bytes 786440 | tf_op jit(solution)/shard_map/ppermute | solution.py:220
  30.0 3.3 %collective-permute-done.2.refs_1_ = bf16[8,128,256]{2,1,0:T(8,128)(2,1)S(1)} collective-permute-done((bf16[8,128,256]{2,1,0:T(8,128)(2,1)S(1)}, bf16[8,128,256]{2,1,0:T(8,128)(2,1)S(1)}, u32[]{:S(2)}, u32[]{:S(2)}) %collective-permute-start.2) | collective-permute-done | bytes 524320 | tf_op jit(solution)/shard_map/ppermute | solution.py:220
  33.3 0.5 shard_map.43
  33.8 3.2 %collective-permute-start.6 = (bf16[4,128,256]{2,1,0:T(8,128)(2,1)S(1)}, bf16[4,128,256]{2,1,0:T(8,128)(2,1)S(1)}, u32[]{:S(2)}, u32[]{:S(2)}) collective-permute-start(bf16[4,128,256]{2,1,0:T(8,128)(2,1)S(1)} %get-tuple-element.40.refs_0_), channel_id=1, source_target_pairs={{0,2},{1,3},{2,0},{3,1},{4,6},{5,7},{6,4},{7,5},{8,10},{9,11},{10,... | collective-permute-start | bytes 786440 | tf_op jit(solution)/shard_map/ppermute | solution.py:220
  37.0 4.2 %collective-permute-done.7.refs_1_ = bf16[4,128,256]{2,1,0:T(8,128)(2,1)S(1)} collective-permute-done((bf16[4,128,256]{2,1,0:T(8,128)(2,1)S(1)}, bf16[4,128,256]{2,1,0:T(8,128)(2,1)S(1)}, u32[]{:S(2)}, u32[]{:S(2)}) %collective-permute-start.7) | collective-permute-done | bytes 262176 | tf_op jit(solution)/shard_map/ppermute | solution.py:220
  41.2 0.4 shard_map.44
  41.6 1.7 %collective-permute-start.9 = (bf16[2,128,256]{2,1,0:T(8,128)(2,1)S(1)}, bf16[2,128,256]{2,1,0:T(8,128)(2,1)S(1)}, u32[]{:S(2)}, u32[]{:S(2)}) collective-permute-start(bf16[2,128,256]{2,1,0:T(8,128)(2,1)S(1)} %get-tuple-element.44), channel_id=1, source_target_pairs={{0,32},{16,48},{32,0},{48,16},{64,96},{80,112},{96,64},{112,80},{1... | collective-permute-start | bytes 393224 | tf_op jit(solution)/shard_map/ppermute | solution.py:220
  43.2 0.8 collective-permute-start.5
  44.1 2.6 %collective-permute-done.9.refs_1_ = bf16[2,128,256]{2,1,0:T(8,128)(2,1)S(1)} collective-permute-done((bf16[2,128,256]{2,1,0:T(8,128)(2,1)S(1)}, bf16[2,128,256]{2,1,0:T(8,128)(2,1)S(1)}, u32[]{:S(2)}, u32[]{:S(2)}) %collective-permute-start.9) | collective-permute-done | bytes 131104 | tf_op jit(solution)/shard_map/ppermute | solution.py:220
  47.0 2.0 %collective-permute-start.13 = (bf16[4,128,256]{2,1,0:T(8,128)(2,1)S(1)}, bf16[4,128,256]{2,1,0:T(8,128)(2,1)S(1)}, u32[]{:S(2)}, u32[]{:S(2)}) collective-permute-start(bf16[4,128,256]{2,1,0:T(8,128)(2,1)S(1)} %shard_map.45.refs_3_.refs_0_), channel_id=1, source_target_pairs={{0,4},{1,5},{2,6},{3,7},{4,0},{5,1},{6,2},{7,3},{8,12},{9,13},{10,... | collective-permute-start | bytes 786440 | tf_op jit(solution)/shard_map/ppermute | solution.py:220
  49.0 0.4 shard_map.46
  49.4 1.6 %collective-permute-start.14 = (bf16[2,128,256]{2,1,0:T(8,128)(2,1)S(1)}, bf16[2,128,256]{2,1,0:T(8,128)(2,1)S(1)}, u32[]{:S(2)}, u32[]{:S(2)}) collective-permute-start(bf16[2,128,256]{2,1,0:T(8,128)(2,1)S(1)} %get-tuple-element.49), channel_id=1, source_target_pairs={{0,32},{16,48},{32,0},{48,16},{64,96},{80,112},{96,64},{112,80},{1... | collective-permute-start | bytes 393224 | tf_op jit(solution)/shard_map/ppermute | solution.py:220
  51.0 0.8 collective-permute-start.4
  51.9 0.4 shard_map.47
  52.2 1.9 %collective-permute-start.12 = (bf16[2,128,256]{2,1,0:T(8,128)(2,1)S(1)}, bf16[2,128,256]{2,1,0:T(8,128)(2,1)S(1)}, u32[]{:S(2)}, u32[]{:S(2)}) collective-permute-start(bf16[2,128,256]{2,1,0:T(8,128)(2,1)S(1)} %get-tuple-element.48), channel_id=1, source_target_pairs={{0,32},{16,48},{32,0},{48,16},{64,96},{80,112},{96,64},{112,80},{1... | collective-permute-start | bytes 393224 | tf_op jit(solution)/shard_map/ppermute | solution.py:220
  54.2 1.4 %collective-permute-done.14.refs_1_ = bf16[2,128,256]{2,1,0:T(8,128)(2,1)S(1)} collective-permute-done((bf16[2,128,256]{2,1,0:T(8,128)(2,1)S(1)}, bf16[2,128,256]{2,1,0:T(8,128)(2,1)S(1)}, u32[]{:S(2)}, u32[]{:S(2)}) %collective-permute-start.14) | collective-permute-done | bytes 131104 | tf_op jit(solution)/shard_map/ppermute | solution.py:220
  55.6 0.4 shard_map.48.refs_4_.refs_0_
  55.9 1.3 %collective-permute-start.16 = (bf16[4,128,256]{2,1,0:T(8,128)(2,1)S(1)}, bf16[4,128,256]{2,1,0:T(8,128)(2,1)S(1)}, u32[]{:S(2)}, u32[]{:S(2)}) collective-permute-start(bf16[4,128,256]{2,1,0:T(8,128)(2,1)S(1)} %shard_map.48.refs_4_.refs_0_), channel_id=1, source_target_pairs={{0,4},{1,5},{2,6},{3,7},{4,0},{5,1},{6,2},{7,3},{8,12},{9,13},{10,... | collective-permute-start | bytes 786440 | tf_op jit(solution)/shard_map/ppermute | solution.py:220
  57.3 0.4 shard_map.49
  57.7 3.0 %collective-permute-start.17 = (bf16[2,128,256]{2,1,0:T(8,128)(2,1)S(1)}, bf16[2,128,256]{2,1,0:T(8,128)(2,1)S(1)}, u32[]{:S(2)}, u32[]{:S(2)}) collective-permute-start(bf16[2,128,256]{2,1,0:T(8,128)(2,1)S(1)} %get-tuple-element.53), channel_id=1, source_target_pairs={{0,64},{16,80},{32,96},{48,112},{64,0},{80,16},{96,32},{112,48},{1... | collective-permute-start | bytes 393224 | tf_op jit(solution)/shard_map/ppermute | solution.py:220
  60.6 0.4 shard_map.50.refs_3_.refs_0_
  61.0 1.2 %collective-permute-start.20 = (bf16[4,128,256]{2,1,0:T(8,128)(2,1)S(1)}, bf16[4,128,256]{2,1,0:T(8,128)(2,1)S(1)}, u32[]{:S(2)}, u32[]{:S(2)}) collective-permute-start(bf16[4,128,256]{2,1,0:T(8,128)(2,1)S(1)} %shard_map.50.refs_3_.refs_0_), channel_id=1, source_target_pairs={{0,4},{1,5},{2,6},{3,7},{4,0},{5,1},{6,2},{7,3},{8,12},{9,13},{10,... | collective-permute-start | bytes 786440 | tf_op jit(solution)/shard_map/ppermute | solution.py:220
  62.2 0.4 shard_map.51
  62.6 1.5 %collective-permute-start.15 = (bf16[2,128,256]{2,1,0:T(8,128)(2,1)S(1)}, bf16[2,128,256]{2,1,0:T(8,128)(2,1)S(1)}, u32[]{:S(2)}, u32[]{:S(2)}) collective-permute-start(bf16[2,128,256]{2,1,0:T(8,128)(2,1)S(1)} %get-tuple-element.52), channel_id=1, source_target_pairs={{0,32},{16,48},{32,0},{48,16},{64,96},{80,112},{96,64},{112,80},{1... | collective-permute-start | bytes 393224 | tf_op jit(solution)/shard_map/ppermute | solution.py:220
  64.1 1.1 %collective-permute-done.17.refs_1_ = bf16[2,128,256]{2,1,0:T(8,128)(2,1)S(1)} collective-permute-done((bf16[2,128,256]{2,1,0:T(8,128)(2,1)S(1)}, bf16[2,128,256]{2,1,0:T(8,128)(2,1)S(1)}, u32[]{:S(2)}, u32[]{:S(2)}) %collective-permute-start.17) | collective-permute-done | bytes 131104 | tf_op jit(solution)/shard_map/ppermute | solution.py:220
  65.2 0.4 shard_map.52.refs_4_.refs_0_
  65.6 3.7 %collective-permute-start.19 = (bf16[4,128,256]{2,1,0:T(8,128)(2,1)S(1)}, bf16[4,128,256]{2,1,0:T(8,128)(2,1)S(1)}, u32[]{:S(2)}, u32[]{:S(2)}) collective-permute-start(bf16[4,128,256]{2,1,0:T(8,128)(2,1)S(1)} %shard_map.52.refs_4_.refs_0_), channel_id=1, source_target_pairs={{0,8},{1,9},{2,10},{3,11},{4,12},{5,13},{6,14},{7,15},{8,0},{9,1},... | collective-permute-start | bytes 786440 | tf_op jit(solution)/shard_map/ppermute | solution.py:220
  69.2 0.4 shard_map.53
  69.6 2.1 %collective-permute-start.22 = (bf16[2,128,256]{2,1,0:T(8,128)(2,1)S(1)}, bf16[2,128,256]{2,1,0:T(8,128)(2,1)S(1)}, u32[]{:S(2)}, u32[]{:S(2)}) collective-permute-start(bf16[2,128,256]{2,1,0:T(8,128)(2,1)S(1)} %get-tuple-element.58), channel_id=1, source_target_pairs={{0,64},{16,80},{32,96},{48,112},{64,0},{80,16},{96,32},{112,48},{1... | collective-permute-start | bytes 393224 | tf_op jit(solution)/shard_map/ppermute | solution.py:220
  71.8 0.4 shard_map.54.refs_4_.refs_0_
  72.1 0.7 collective-permute-start.18
  72.9 0.4 shard_map.55
  73.2 1.2 %collective-permute-start.21 = (bf16[2,128,256]{2,1,0:T(8,128)(2,1)S(1)}, bf16[2,128,256]{2,1,0:T(8,128)(2,1)S(1)}, u32[]{:S(2)}, u32[]{:S(2)}) collective-permute-start(bf16[2,128,256]{2,1,0:T(8,128)(2,1)S(1)} %get-tuple-element.57), channel_id=1, source_target_pairs={{0,64},{16,80},{32,96},{48,112},{64,0},{80,16},{96,32},{112,48},{1... | collective-permute-start | bytes 393224 | tf_op jit(solution)/shard_map/ppermute | solution.py:220
  74.5 1.9 %collective-permute-done.22.refs_1_ = bf16[2,128,256]{2,1,0:T(8,128)(2,1)S(1)} collective-permute-done((bf16[2,128,256]{2,1,0:T(8,128)(2,1)S(1)}, bf16[2,128,256]{2,1,0:T(8,128)(2,1)S(1)}, u32[]{:S(2)}, u32[]{:S(2)}) %collective-permute-start.22) | collective-permute-done | bytes 131104 | tf_op jit(solution)/shard_map/ppermute | solution.py:220
  76.7 1.9 %collective-permute-start.24 = (bf16[4,128,256]{2,1,0:T(8,128)(2,1)S(1)}, bf16[4,128,256]{2,1,0:T(8,128)(2,1)S(1)}, u32[]{:S(2)}, u32[]{:S(2)}) collective-permute-start(bf16[4,128,256]{2,1,0:T(8,128)(2,1)S(1)} %shard_map.56.refs_6_.refs_0_), channel_id=1, source_target_pairs={{0,8},{1,9},{2,10},{3,11},{4,12},{5,13},{6,14},{7,15},{8,0},{9,1},... | collective-permute-start | bytes 786440 | tf_op jit(solution)/shard_map/ppermute | solution.py:220
  78.6 1.1 %collective-permute-done.21.refs_1_ = bf16[2,128,256]{2,1,0:T(8,128)(2,1)S(1)} collective-permute-done((bf16[2,128,256]{2,1,0:T(8,128)(2,1)S(1)}, bf16[2,128,256]{2,1,0:T(8,128)(2,1)S(1)}, u32[]{:S(2)}, u32[]{:S(2)}) %collective-permute-start.21) | collective-permute-done | bytes 131104 | tf_op jit(solution)/shard_map/ppermute | solution.py:220
  80.2 0.4 shard_map.58.refs_4_
  80.5 1.5 %collective-permute-done.18.refs_1_ = bf16[4,128,256]{2,1,0:T(8,128)(2,1)S(1)} collective-permute-done((bf16[4,128,256]{2,1,0:T(8,128)(2,1)S(1)}, bf16[4,128,256]{2,1,0:T(8,128)(2,1)S(1)}, u32[]{:S(2)}, u32[]{:S(2)}) %collective-permute-start.18) | collective-permute-done | bytes 262176 | tf_op jit(solution)/shard_map/ppermute | solution.py:220
  82.1 0.4 shard_map.59
  82.4 2.3 %collective-permute-start.23 = (bf16[2,128,256]{2,1,0:T(8,128)(2,1)S(1)}, bf16[2,128,256]{2,1,0:T(8,128)(2,1)S(1)}, u32[]{:S(2)}, u32[]{:S(2)}) collective-permute-start(bf16[2,128,256]{2,1,0:T(8,128)(2,1)S(1)} %get-tuple-element.60), channel_id=1, source_target_pairs={{0,64},{16,80},{32,96},{48,112},{64,0},{80,16},{96,32},{112,48},{1... | collective-permute-start | bytes 393224 | tf_op jit(solution)/shard_map/ppermute | solution.py:220
  84.7 4.7 %collective-permute-start.26 = (bf16[4,128,256]{2,1,0:T(8,128)(2,1)S(1)}, bf16[4,128,256]{2,1,0:T(8,128)(2,1)S(1)}, u32[]{:S(2)}, u32[]{:S(2)}) collective-permute-start(bf16[4,128,256]{2,1,0:T(8,128)(2,1)S(1)} %shard_map.57.refs_6_.refs_0_), channel_id=1, source_target_pairs={{0,8},{1,9},{2,10},{3,11},{4,12},{5,13},{6,14},{7,15},{8,0},{9,1},... | collective-permute-start | bytes 786440 | tf_op jit(solution)/shard_map/ppermute | solution.py:220
  89.7 0.8 collective-permute-done.24.refs_1_
  90.5 0.4 shard_map.60.refs_6_
  90.9 0.4 shard_map.61.refs_6_.refs_0_
  91.2 1.6 %collective-permute-start.25 = (bf16[4,128,256]{2,1,0:T(8,128)(2,1)S(1)}, bf16[4,128,256]{2,1,0:T(8,128)(2,1)S(1)}, u32[]{:S(2)}, u32[]{:S(2)}) collective-permute-start(bf16[4,128,256]{2,1,0:T(8,128)(2,1)S(1)} %shard_map.61.refs_6_.refs_0_), channel_id=1, source_target_pairs={{0,8},{1,9},{2,10},{3,11},{4,12},{5,13},{6,14},{7,15},{8,0},{9,1},... | collective-permute-start | bytes 786440 | tf_op jit(solution)/shard_map/ppermute | solution.py:220
  93.1 2.8 %collective-permute-done.26.refs_1_ = bf16[4,128,256]{2,1,0:T(8,128)(2,1)S(1)} collective-permute-done((bf16[4,128,256]{2,1,0:T(8,128)(2,1)S(1)}, bf16[4,128,256]{2,1,0:T(8,128)(2,1)S(1)}, u32[]{:S(2)}, u32[]{:S(2)}) %collective-permute-start.26) | collective-permute-done | bytes 262176 | tf_op jit(solution)/shard_map/ppermute | solution.py:220
  95.9 0.4 shard_map.62.refs_6_.k._
  96.2 1.4 %shard_map.64._ = bf16[2,1024,256]{2,1,0:T(8,128)(2,1)} custom-call(bf16[2,8,1024,128]{3,2,1,0:T(8,128)(2,1)S(1)} %bitcast.4, bf16[4,128,256]{2,1,0:T(8,128)(2,1)S(1)} %shard_map.62.refs_6_.k._, bf16[4,128,256]{2,1,0:T(8,128)(2,1)S(1)} %collective-permute-done.28.c, bf16[4,128,256]{2,1,0:T(8,128)(2,1)S(1)} %shard_map.62.refs_6_.k._), custom_call_target="tpu_custom_call" | custom-call | flops 536870912 | bytes 2621440 | tf_op jit(solution)/shard_map/pallas_call | solution.py:199
  97.7 1.5 %collective-permute-done.25.refs_1_ = bf16[4,128,256]{2,1,0:T(8,128)(2,1)S(1)} collective-permute-done((bf16[4,128,256]{2,1,0:T(8,128)(2,1)S(1)}, bf16[4,128,256]{2,1,0:T(8,128)(2,1)S(1)}, u32[]{:S(2)}, u32[]{:S(2)}) %collective-permute-start.25) | collective-permute-done | bytes 262176 | tf_op jit(solution)/shard_map/ppermute | solution.py:220
  99.2 0.4 shard_map.63.k
  99.6 1.4 %shard_map.65 = bf16[2,1024,256]{2,1,0:T(8,128)(2,1)} custom-call(bf16[2,8,1024,128]{3,2,1,0:T(8,128)(2,1)S(1)} %bitcast.5, bf16[4,128,256]{2,1,0:T(8,128)(2,1)S(1)} %shard_map.63.k, bf16[4,128,256]{2,1,0:T(8,128)(2,1)S(1)} %collective-permute-done.27.c, bf16[2,1024,256]{2,1,0:T(8,128)(2,1)} %shard_map.64._), custom_call_target="tpu_custom_call", output_to_operand_aliasing={{}: (3, {})} | custom-call | flops 536870912 | bytes 2621440 | tf_op jit(solution)/shard_map/pallas_call | solution.py:199
  (25 shorter events, 2.0 us)
Async XLA Ops:
  4.7 2.0 %collective-permute-start.1 = (bf16[8,128,256]{2,1,0:T(8,128)(2,1)S(1)}, bf16[8,128,256]{2,1,0:T(8,128)(2,1)S(1)}, u32[]{:S(2)}, u32[]{:S(2)}) collective-permute-start(bf16[8,128,256]{2,1,0:T(8,128)(2,1)S(1)} %get-tuple-element.35._.refs_0_), channel_id=1, source_target_pairs={{0,1},{1,0},{2,3},{3,2},{4,5},{5,4},{6,7},{7,6},{8,9},{9,8},{10,11... | collective-permute-start | bytes 1572872 | tf_op jit(solution)/shard_map/ppermute | solution.py:220
  4.8 4.1 %collective-permute-start = (bf16[8,128,256]{2,1,0:T(8,128)(2,1)S(1)}, bf16[8,128,256]{2,1,0:T(8,128)(2,1)S(1)}, u32[]{:S(2)}, u32[]{:S(2)}) collective-permute-start(bf16[8,128,256]{2,1,0:T(8,128)(2,1)S(1)} %get-tuple-element.33.refs_0_), channel_id=1, source_target_pairs={{0,1},{1,0},{2,3},{3,2},{4,5},{5,4},{6,7},{7,6},{8,9},{9,8},{10,11... | collective-permute-start | bytes 1572872 | tf_op jit(solution)/shard_map/ppermute | solution.py:220
  7.2 14.8 %collective-permute-start.3 = (bf16[8,128,256]{2,1,0:T(8,128)(2,1)S(1)}, bf16[8,128,256]{2,1,0:T(8,128)(2,1)S(1)}, u32[]{:S(2)}, u32[]{:S(2)}) collective-permute-start(bf16[8,128,256]{2,1,0:T(8,128)(2,1)S(1)} %shard_map.39.refs_3_.refs_0_), channel_id=1, source_target_pairs={{0,16},{16,0},{32,48},{48,32},{64,80},{80,64},{96,112},{112,96},{1... | collective-permute-start | bytes 1572872 | tf_op jit(solution)/shard_map/ppermute | solution.py:220
  11.0 30.2 %collective-permute-start.8 = (bf16[12,2,64,256]{3,2,1,0:T(8,128)(2,1)S(1)}, bf16[12,2,64,256]{3,2,1,0:T(8,128)(2,1)S(1)}, u32[]{:S(2)}, u32[]{:S(2)}) collective-permute-start(bf16[12,2,64,256]{3,2,1,0:T(8,128)(2,1)S(1)} %get-tuple-element.42), channel_id=1, source_target_pairs={{0,32},{16,48},{32,0},{48,16},{64,96},{80,112},{96,64},{112,80},{1... | collective-permute-start | bytes 2359304 | tf_op jit(solution)/shard_map/ppermute | solution.py:220
  12.7 20.6 %collective-permute-start.2 = (bf16[8,128,256]{2,1,0:T(8,128)(2,1)S(1)}, bf16[8,128,256]{2,1,0:T(8,128)(2,1)S(1)}, u32[]{:S(2)}, u32[]{:S(2)}) collective-permute-start(bf16[8,128,256]{2,1,0:T(8,128)(2,1)S(1)} %shard_map.40._.refs_0_), channel_id=1, source_target_pairs={{0,16},{16,0},{32,48},{48,32},{64,80},{80,64},{96,112},{112,96},{1... | collective-permute-start | bytes 1572872 | tf_op jit(solution)/shard_map/ppermute | solution.py:220
  22.6 18.6 %collective-permute-start.7 = (bf16[4,128,256]{2,1,0:T(8,128)(2,1)S(1)}, bf16[4,128,256]{2,1,0:T(8,128)(2,1)S(1)}, u32[]{:S(2)}, u32[]{:S(2)}) collective-permute-start(bf16[4,128,256]{2,1,0:T(8,128)(2,1)S(1)} %get-tuple-element.41.refs_0_), channel_id=1, source_target_pairs={{0,2},{1,3},{2,0},{3,1},{4,6},{5,7},{6,4},{7,5},{8,10},{9,11},{10,... | collective-permute-start | bytes 786440 | tf_op jit(solution)/shard_map/ppermute | solution.py:220
  25.8 18.3 %collective-permute-start.10 = (bf16[4,2,64,256]{3,2,1,0:T(8,128)(2,1)S(1)}, bf16[4,2,64,256]{3,2,1,0:T(8,128)(2,1)S(1)}, u32[]{:S(2)}, u32[]{:S(2)}) collective-permute-start(bf16[4,2,64,256]{3,2,1,0:T(8,128)(2,1)S(1)} %get-tuple-element.36.refs_3_), channel_id=1, source_target_pairs={{0,64},{16,80},{32,96},{48,112},{64,0},{80,16},{96,32},{112,48},{1... | collective-permute-start | bytes 786440 | tf_op jit(solution)/shard_map/ppermute | solution.py:220
  29.0 15.1 %collective-permute-start.11 = (bf16[4,2,64,256]{3,2,1,0:T(8,128)(2,1)S(1)}, bf16[4,2,64,256]{3,2,1,0:T(8,128)(2,1)S(1)}, u32[]{:S(2)}, u32[]{:S(2)}) collective-permute-start(bf16[4,2,64,256]{3,2,1,0:T(8,128)(2,1)S(1)} %get-tuple-element.45), channel_id=1, source_target_pairs={{0,96},{16,112},{32,64},{48,80},{64,32},{80,48},{96,0},{112,16},{1... | collective-permute-start | bytes 786440 | tf_op jit(solution)/shard_map/ppermute | solution.py:220
  33.8 15.2 %collective-permute-start.6 = (bf16[4,128,256]{2,1,0:T(8,128)(2,1)S(1)}, bf16[4,128,256]{2,1,0:T(8,128)(2,1)S(1)}, u32[]{:S(2)}, u32[]{:S(2)}) collective-permute-start(bf16[4,128,256]{2,1,0:T(8,128)(2,1)S(1)} %get-tuple-element.40.refs_0_), channel_id=1, source_target_pairs={{0,2},{1,3},{2,0},{3,1},{4,6},{5,7},{6,4},{7,5},{8,10},{9,11},{10,... | collective-permute-start | bytes 786440 | tf_op jit(solution)/shard_map/ppermute | solution.py:220
  41.6 5.0 %collective-permute-start.9 = (bf16[2,128,256]{2,1,0:T(8,128)(2,1)S(1)}, bf16[2,128,256]{2,1,0:T(8,128)(2,1)S(1)}, u32[]{:S(2)}, u32[]{:S(2)}) collective-permute-start(bf16[2,128,256]{2,1,0:T(8,128)(2,1)S(1)} %get-tuple-element.44), channel_id=1, source_target_pairs={{0,32},{16,48},{32,0},{48,16},{64,96},{80,112},{96,64},{112,80},{1... | collective-permute-start | bytes 393224 | tf_op jit(solution)/shard_map/ppermute | solution.py:220
  43.2 8.6 %collective-permute-start.5 = (bf16[4,128,256]{2,1,0:T(8,128)(2,1)S(1)}, bf16[4,128,256]{2,1,0:T(8,128)(2,1)S(1)}, u32[]{:S(2)}, u32[]{:S(2)}) collective-permute-start(bf16[4,128,256]{2,1,0:T(8,128)(2,1)S(1)} %get-tuple-element.38.refs_3_.refs_0_), channel_id=1, source_target_pairs={{0,2},{1,3},{2,0},{3,1},{4,6},{5,7},{6,4},{7,5},{8,10},{9,11},{10,... | collective-permute-start | bytes 786440 | tf_op jit(solution)/shard_map/ppermute | solution.py:220
  47.0 10.3 %collective-permute-start.13 = (bf16[4,128,256]{2,1,0:T(8,128)(2,1)S(1)}, bf16[4,128,256]{2,1,0:T(8,128)(2,1)S(1)}, u32[]{:S(2)}, u32[]{:S(2)}) collective-permute-start(bf16[4,128,256]{2,1,0:T(8,128)(2,1)S(1)} %shard_map.45.refs_3_.refs_0_), channel_id=1, source_target_pairs={{0,4},{1,5},{2,6},{3,7},{4,0},{5,1},{6,2},{7,3},{8,12},{9,13},{10,... | collective-permute-start | bytes 786440 | tf_op jit(solution)/shard_map/ppermute | solution.py:220
  49.4 6.2 %collective-permute-start.14 = (bf16[2,128,256]{2,1,0:T(8,128)(2,1)S(1)}, bf16[2,128,256]{2,1,0:T(8,128)(2,1)S(1)}, u32[]{:S(2)}, u32[]{:S(2)}) collective-permute-start(bf16[2,128,256]{2,1,0:T(8,128)(2,1)S(1)} %get-tuple-element.49), channel_id=1, source_target_pairs={{0,32},{16,48},{32,0},{48,16},{64,96},{80,112},{96,64},{112,80},{1... | collective-permute-start | bytes 393224 | tf_op jit(solution)/shard_map/ppermute | solution.py:220
  51.0 11.2 %collective-permute-start.4 = (bf16[4,128,256]{2,1,0:T(8,128)(2,1)S(1)}, bf16[4,128,256]{2,1,0:T(8,128)(2,1)S(1)}, u32[]{:S(2)}, u32[]{:S(2)}) collective-permute-start(bf16[4,128,256]{2,1,0:T(8,128)(2,1)S(1)} %get-tuple-element.39.refs_4_.refs_0_), channel_id=1, source_target_pairs={{0,2},{1,3},{2,0},{3,1},{4,6},{5,7},{6,4},{7,5},{8,10},{9,11},{10,... | collective-permute-start | bytes 786440 | tf_op jit(solution)/shard_map/ppermute | solution.py:220
  52.2 8.4 %collective-permute-start.12 = (bf16[2,128,256]{2,1,0:T(8,128)(2,1)S(1)}, bf16[2,128,256]{2,1,0:T(8,128)(2,1)S(1)}, u32[]{:S(2)}, u32[]{:S(2)}) collective-permute-start(bf16[2,128,256]{2,1,0:T(8,128)(2,1)S(1)} %get-tuple-element.48), channel_id=1, source_target_pairs={{0,32},{16,48},{32,0},{48,16},{64,96},{80,112},{96,64},{112,80},{1... | collective-permute-start | bytes 393224 | tf_op jit(solution)/shard_map/ppermute | solution.py:220
  55.9 13.3 %collective-permute-start.16 = (bf16[4,128,256]{2,1,0:T(8,128)(2,1)S(1)}, bf16[4,128,256]{2,1,0:T(8,128)(2,1)S(1)}, u32[]{:S(2)}, u32[]{:S(2)}) collective-permute-start(bf16[4,128,256]{2,1,0:T(8,128)(2,1)S(1)} %shard_map.48.refs_4_.refs_0_), channel_id=1, source_target_pairs={{0,4},{1,5},{2,6},{3,7},{4,0},{5,1},{6,2},{7,3},{8,12},{9,13},{10,... | collective-permute-start | bytes 786440 | tf_op jit(solution)/shard_map/ppermute | solution.py:220
  57.7 7.5 %collective-permute-start.17 = (bf16[2,128,256]{2,1,0:T(8,128)(2,1)S(1)}, bf16[2,128,256]{2,1,0:T(8,128)(2,1)S(1)}, u32[]{:S(2)}, u32[]{:S(2)}) collective-permute-start(bf16[2,128,256]{2,1,0:T(8,128)(2,1)S(1)} %get-tuple-element.53), channel_id=1, source_target_pairs={{0,64},{16,80},{32,96},{48,112},{64,0},{80,16},{96,32},{112,48},{1... | collective-permute-start | bytes 393224 | tf_op jit(solution)/shard_map/ppermute | solution.py:220
  61.0 11.9 %collective-permute-start.20 = (bf16[4,128,256]{2,1,0:T(8,128)(2,1)S(1)}, bf16[4,128,256]{2,1,0:T(8,128)(2,1)S(1)}, u32[]{:S(2)}, u32[]{:S(2)}) collective-permute-start(bf16[4,128,256]{2,1,0:T(8,128)(2,1)S(1)} %shard_map.50.refs_3_.refs_0_), channel_id=1, source_target_pairs={{0,4},{1,5},{2,6},{3,7},{4,0},{5,1},{6,2},{7,3},{8,12},{9,13},{10,... | collective-permute-start | bytes 786440 | tf_op jit(solution)/shard_map/ppermute | solution.py:220
  62.6 9.2 %collective-permute-start.15 = (bf16[2,128,256]{2,1,0:T(8,128)(2,1)S(1)}, bf16[2,128,256]{2,1,0:T(8,128)(2,1)S(1)}, u32[]{:S(2)}, u32[]{:S(2)}) collective-permute-start(bf16[2,128,256]{2,1,0:T(8,128)(2,1)S(1)} %get-tuple-element.52), channel_id=1, source_target_pairs={{0,32},{16,48},{32,0},{48,16},{64,96},{80,112},{96,64},{112,80},{1... | collective-permute-start | bytes 393224 | tf_op jit(solution)/shard_map/ppermute | solution.py:220
  65.6 14.6 %collective-permute-start.19 = (bf16[4,128,256]{2,1,0:T(8,128)(2,1)S(1)}, bf16[4,128,256]{2,1,0:T(8,128)(2,1)S(1)}, u32[]{:S(2)}, u32[]{:S(2)}) collective-permute-start(bf16[4,128,256]{2,1,0:T(8,128)(2,1)S(1)} %shard_map.52.refs_4_.refs_0_), channel_id=1, source_target_pairs={{0,8},{1,9},{2,10},{3,11},{4,12},{5,13},{6,14},{7,15},{8,0},{9,1},... | collective-permute-start | bytes 786440 | tf_op jit(solution)/shard_map/ppermute | solution.py:220
  69.6 6.7 %collective-permute-start.22 = (bf16[2,128,256]{2,1,0:T(8,128)(2,1)S(1)}, bf16[2,128,256]{2,1,0:T(8,128)(2,1)S(1)}, u32[]{:S(2)}, u32[]{:S(2)}) collective-permute-start(bf16[2,128,256]{2,1,0:T(8,128)(2,1)S(1)} %get-tuple-element.58), channel_id=1, source_target_pairs={{0,64},{16,80},{32,96},{48,112},{64,0},{80,16},{96,32},{112,48},{1... | collective-permute-start | bytes 393224 | tf_op jit(solution)/shard_map/ppermute | solution.py:220
  72.1 9.9 %collective-permute-start.18 = (bf16[4,128,256]{2,1,0:T(8,128)(2,1)S(1)}, bf16[4,128,256]{2,1,0:T(8,128)(2,1)S(1)}, u32[]{:S(2)}, u32[]{:S(2)}) collective-permute-start(bf16[4,128,256]{2,1,0:T(8,128)(2,1)S(1)} %shard_map.54.refs_4_.refs_0_), channel_id=1, source_target_pairs={{0,4},{1,5},{2,6},{3,7},{4,0},{5,1},{6,2},{7,3},{8,12},{9,13},{10,... | collective-permute-start | bytes 786440 | tf_op jit(solution)/shard_map/ppermute | solution.py:220
  73.2 6.6 %collective-permute-start.21 = (bf16[2,128,256]{2,1,0:T(8,128)(2,1)S(1)}, bf16[2,128,256]{2,1,0:T(8,128)(2,1)S(1)}, u32[]{:S(2)}, u32[]{:S(2)}) collective-permute-start(bf16[2,128,256]{2,1,0:T(8,128)(2,1)S(1)} %get-tuple-element.57), channel_id=1, source_target_pairs={{0,64},{16,80},{32,96},{48,112},{64,0},{80,16},{96,32},{112,48},{1... | collective-permute-start | bytes 393224 | tf_op jit(solution)/shard_map/ppermute | solution.py:220
  76.7 13.8 %collective-permute-start.24 = (bf16[4,128,256]{2,1,0:T(8,128)(2,1)S(1)}, bf16[4,128,256]{2,1,0:T(8,128)(2,1)S(1)}, u32[]{:S(2)}, u32[]{:S(2)}) collective-permute-start(bf16[4,128,256]{2,1,0:T(8,128)(2,1)S(1)} %shard_map.56.refs_6_.refs_0_), channel_id=1, source_target_pairs={{0,8},{1,9},{2,10},{3,11},{4,12},{5,13},{6,14},{7,15},{8,0},{9,1},... | collective-permute-start | bytes 786440 | tf_op jit(solution)/shard_map/ppermute | solution.py:220
  82.4 13.8 %copy-start = (bf16[1,2,8,1024,128]{4,3,2,1,0:T(8,128)(2,1)S(1)}, bf16[1,2,8,1024,128]{4,3,2,1,0:T(8,128)(2,1)}, u32[]{:S(2)}) copy-start(bf16[1,2,8,1024,128]{4,3,2,1,0:T(8,128)(2,1)} %param.5) | copy-start | bytes 12582916
  82.4 8.4 %collective-permute-start.23 = (bf16[2,128,256]{2,1,0:T(8,128)(2,1)S(1)}, bf16[2,128,256]{2,1,0:T(8,128)(2,1)S(1)}, u32[]{:S(2)}, u32[]{:S(2)}) collective-permute-start(bf16[2,128,256]{2,1,0:T(8,128)(2,1)S(1)} %get-tuple-element.60), channel_id=1, source_target_pairs={{0,64},{16,80},{32,96},{48,112},{64,0},{80,16},{96,32},{112,48},{1... | collective-permute-start | bytes 393224 | tf_op jit(solution)/shard_map/ppermute | solution.py:220
  84.7 11.2 %collective-permute-start.26 = (bf16[4,128,256]{2,1,0:T(8,128)(2,1)S(1)}, bf16[4,128,256]{2,1,0:T(8,128)(2,1)S(1)}, u32[]{:S(2)}, u32[]{:S(2)}) collective-permute-start(bf16[4,128,256]{2,1,0:T(8,128)(2,1)S(1)} %shard_map.57.refs_6_.refs_0_), channel_id=1, source_target_pairs={{0,8},{1,9},{2,10},{3,11},{4,12},{5,13},{6,14},{7,15},{8,0},{9,1},... | collective-permute-start | bytes 786440 | tf_op jit(solution)/shard_map/ppermute | solution.py:220
  89.4 6.8 %collective-permute-start.28 = (bf16[4,128,256]{2,1,0:T(8,128)(2,1)S(1)}, bf16[4,128,256]{2,1,0:T(8,128)(2,1)S(1)}, u32[]{:S(2)}, u32[]{:S(2)}) collective-permute-start(bf16[4,128,256]{2,1,0:T(8,128)(2,1)S(1)} %shard_map.58.refs_4_), channel_id=1, source_target_pairs={{0,16},{16,0},{32,48},{48,32},{64,80},{80,64},{96,112},{112,96},{1... | collective-permute-start | bytes 786440 | tf_op jit(solution)/shard_map/ppermute | solution.py:220
  91.2 8.0 %collective-permute-start.25 = (bf16[4,128,256]{2,1,0:T(8,128)(2,1)S(1)}, bf16[4,128,256]{2,1,0:T(8,128)(2,1)S(1)}, u32[]{:S(2)}, u32[]{:S(2)}) collective-permute-start(bf16[4,128,256]{2,1,0:T(8,128)(2,1)S(1)} %shard_map.61.refs_6_.refs_0_), channel_id=1, source_target_pairs={{0,8},{1,9},{2,10},{3,11},{4,12},{5,13},{6,14},{7,15},{8,0},{9,1},... | collective-permute-start | bytes 786440 | tf_op jit(solution)/shard_map/ppermute | solution.py:220
  92.8 6.7 %collective-permute-start.27 = (bf16[4,128,256]{2,1,0:T(8,128)(2,1)S(1)}, bf16[4,128,256]{2,1,0:T(8,128)(2,1)S(1)}, u32[]{:S(2)}, u32[]{:S(2)}) collective-permute-start(bf16[4,128,256]{2,1,0:T(8,128)(2,1)S(1)} %shard_map.60.refs_6_), channel_id=1, source_target_pairs={{0,16},{16,0},{32,48},{48,32},{64,80},{80,64},{96,112},{112,96},{1... | collective-permute-start | bytes 786440 | tf_op jit(solution)/shard_map/ppermute | solution.py:220
where the time goes:
time: 101 us
  starting transfers between devices  49.7 us (49%)
  waiting for transfers between devices  31.4 us (31%)
  Pallas kernels  19.7 us (20%)
    ppermute x29, starting transfers between devices, swapped(): lax.ppermute(shard, axis, [(i, i ^ mask) for i in range(lax.axis_size(axi...  49.7 us
    ppermute x29, waiting for transfers between devices, swapped(): lax.ppermute(shard, axis, [(i, i ^ mask) for i in range(lax.axis_size(axi...  31.4 us
    pallas_call x27, Pallas kernels, call(): pl.pallas_call(body, out_shape=[jax.ShapeDtypeStruct(s, BF16) for s in ou...  16.8 us
    pallas_call x2, Pallas kernels, evaluated(): pl.pallas_call(body, out_shape=jax.ShapeDtypeStruct((boxes, points, shots...  2.89 us
  transfers between devices with their start and end apart: 29, of which 13 were waited for; matrix products, arithmetic and copies ran while one was open for 0% of the time, Pallas kernels for 13%

commit v1 on v0

--- a/solution.py
+++ b/solution.py
@@ -326,7 +326,7 @@
     got1, got2, got3 = swapped(send1, "src", 2), swapped(send2, "src", 4), swapped(send3, "src", 6)
     do5(0, ()), do5(1, ())
     do6(P0, (got1,)), do7(P0, (got2, got3)), do6(P1), do6(Q0), do7(P1), do8(P0), do7(Q0), do6(Q1)
-    do9(P0), do8(P1), do7(Q1), do8(Q0), do9(P1), do9(Q0), do10(P0), do8(Q1)
+    do9(P0), do8(P1), do7(Q1), do8(Q0), do9(P1), do9(Q0), do8(Q1), do10(P0)
     do10(P1), do9(Q1), do10(Q0), finish(0), do10(Q1), finish(1)
     field = fields[-1]
     return field[None]

time: 101 us -> 103 us (1.020)
  waiting for transfers between devices: 31.4 us -> 38 us
  starting transfers between devices: 49.7 us -> 44.4 us
    ppermute x29, waiting for transfers between devices: 31.4 us -> 38 us  [swapped(): lax.ppermute(shard, axis, [(i, i ^ mask) for i in range(lax.axis_size(axi...]
    ppermute x29, starting transfers between devices: 49.7 us -> 44.4 us  [swapped(): lax.ppermute(shard, axis, [(i, i ^ mask) for i in range(lax.axis_size(axi...]
  transfers between devices with their start and end apart: 29 -> 29, of which waited for: 13 -> 12; matrix products, arithmetic and copies ran while one was open for 0% -> 0% of each run, Pallas kernels for 13% -> 13%
where the time goes in v1:
time: 103 us
  starting transfers between devices  44.4 us (43%)
  waiting for transfers between devices  38 us (37%)
  Pallas kernels  19.7 us (19%)
    ppermute x29, starting transfers between devices, swapped(): lax.ppermute(shard, axis, [(i, i ^ mask) for i in range(lax.axis_size(axi...  44.4 us
    ppermute x29, waiting for transfers between devices, swapped(): lax.ppermute(shard, axis, [(i, i ^ mask) for i in range(lax.axis_size(axi...  38 us
    pallas_call x27, Pallas kernels, call(): pl.pallas_call(body, out_shape=[jax.ShapeDtypeStruct(s, BF16) for s in ou...  16.8 us
    pallas_call x2, Pallas kernels, evaluated(): pl.pallas_call(body, out_shape=jax.ShapeDtypeStruct((boxes, points, shots...  2.89 us
  transfers between devices with their start and end apart: 29, of which 12 were waited for; matrix products, arithmetic and copies ran while one was open for 0% of the time, Pallas kernels for 13%

profile of v1, /device:TPU:0, one launch (start us, length us, event | category | flops | bytes accessed | tf_op | source)
XLA Modules:
  0.0 102.5 jit_solution(3576927780727280829)
XLA Ops:
  0.0 4.7 %shard_map.37 = (bf16[8,128,256]{2,1,0:T(8,128)(2,1)S(1)}, bf16[8,128,256]{2,1,0:T(8,128)(2,1)S(1)}, bf16[16,3,64,256]{3,2,1,0:T(8,128)(2,1)S(1)}) custom-call(bf16[16,128,256]{2,1,0:T(8,128)(2,1)} %bitcast.9, bf16[16,11,64,256]{3,2,1,0:T(8,128)(2,1)} %bitcast.6), custom_call_target="tpu_custom_call" | custom-call | bytes 1 | tf_op jit(solution)/shard_map/pallas_call | solution.py:37
  4.8 0.5 collective-permute-start
  5.3 1.1 %shard_map.38 = (bf16[4,2,64,256]{3,2,1,0:T(8,128)(2,1)S(1)}, bf16[4,2,64,256]{3,2,1,0:T(8,128)(2,1)S(1)}) custom-call(bf16[16,11,64,256]{3,2,1,0:T(8,128)(2,1)} %bitcast.7, bf16[8,128,256]{2,1,0:T(8,128)(2,1)S(1)} %get-tuple-element.35._.refs_0_), custom_call_target="tpu_custom_call" | custom-call | bytes 1 | tf_op jit(solution)/shard_map/pallas_call | solution.py:37
  6.7 0.5 shard_map.39.refs_3_.refs_0_
  7.2 1.7 %collective-permute-start.3 = (bf16[8,128,256]{2,1,0:T(8,128)(2,1)S(1)}, bf16[8,128,256]{2,1,0:T(8,128)(2,1)S(1)}, u32[]{:S(2)}, u32[]{:S(2)}) collective-permute-start(bf16[8,128,256]{2,1,0:T(8,128)(2,1)S(1)} %shard_map.39.refs_3_.refs_0_), channel_id=1, source_target_pairs={{0,16},{16,0},{32,48},{48,32},{64,80},{80,64},{96,112},{112,96},{1... | collective-permute-start | bytes 1572872 | tf_op jit(solution)/shard_map/ppermute | solution.py:220
  8.9 0.5 shard_map.40._.refs_0_
  9.4 1.6 %shard_map.41 = (bf16[8,2,64,256]{3,2,1,0:T(8,128)(2,1)S(1)}, bf16[12,2,64,256]{3,2,1,0:T(8,128)(2,1)S(1)}, bf16[4,2,64,256]{3,2,1,0:T(8,128)(2,1)S(1)}) custom-call(bf16[16,11,64,256]{3,2,1,0:T(8,128)(2,1)} %bitcast.8, bf16[8,128,256]{2,1,0:T(8,128)(2,1)S(1)} %shard_map.40._.refs_0_), custom_call_target="tpu_custom_call" | custom-call | bytes 1 | tf_op jit(solution)/shard_map/pallas_call | solution.py:37
  11.0 1.7 %collective-permute-start.8 = (bf16[12,2,64,256]{3,2,1,0:T(8,128)(2,1)S(1)}, bf16[12,2,64,256]{3,2,1,0:T(8,128)(2,1)S(1)}, u32[]{:S(2)}, u32[]{:S(2)}) collective-permute-start(bf16[12,2,64,256]{3,2,1,0:T(8,128)(2,1)S(1)} %get-tuple-element.42), channel_id=1, source_target_pairs={{0,32},{16,48},{32,0},{48,16},{64,96},{80,112},{96,64},{112,80},{1... | collective-permute-start | bytes 2359304 | tf_op jit(solution)/shard_map/ppermute | solution.py:220
  12.7 0.5 collective-permute-start.2
  13.2 8.9 %collective-permute-done.3.refs_1_ = bf16[8,128,256]{2,1,0:T(8,128)(2,1)S(1)} collective-permute-done((bf16[8,128,256]{2,1,0:T(8,128)(2,1)S(1)}, bf16[8,128,256]{2,1,0:T(8,128)(2,1)S(1)}, u32[]{:S(2)}, u32[]{:S(2)}) %collective-permute-start.3) | collective-permute-done | bytes 524320 | tf_op jit(solution)/shard_map/ppermute | solution.py:220
  22.1 0.5 shard_map.42
  22.6 3.2 %collective-permute-start.7 = (bf16[4,128,256]{2,1,0:T(8,128)(2,1)S(1)}, bf16[4,128,256]{2,1,0:T(8,128)(2,1)S(1)}, u32[]{:S(2)}, u32[]{:S(2)}) collective-permute-start(bf16[4,128,256]{2,1,0:T(8,128)(2,1)S(1)} %get-tuple-element.41.refs_0_), channel_id=1, source_target_pairs={{0,2},{1,3},{2,0},{3,1},{4,6},{5,7},{6,4},{7,5},{8,10},{9,11},{10,... | collective-permute-start | bytes 786440 | tf_op jit(solution)/shard_map/ppermute | solution.py:220
  25.8 3.2 %collective-permute-start.10 = (bf16[4,2,64,256]{3,2,1,0:T(8,128)(2,1)S(1)}, bf16[4,2,64,256]{3,2,1,0:T(8,128)(2,1)S(1)}, u32[]{:S(2)}, u32[]{:S(2)}) collective-permute-start(bf16[4,2,64,256]{3,2,1,0:T(8,128)(2,1)S(1)} %get-tuple-element.36.refs_3_), channel_id=1, source_target_pairs={{0,64},{16,80},{32,96},{48,112},{64,0},{80,16},{96,32},{112,48},{1... | collective-permute-start | bytes 786440 | tf_op jit(solution)/shard_map/ppermute | solution.py:220
  29.0 1.0 %collective-permute-start.11 = (bf16[4,2,64,256]{3,2,1,0:T(8,128)(2,1)S(1)}, bf16[4,2,64,256]{3,2,1,0:T(8,128)(2,1)S(1)}, u32[]{:S(2)}, u32[]{:S(2)}) collective-permute-start(bf16[4,2,64,256]{3,2,1,0:T(8,128)(2,1)S(1)} %get-tuple-element.45), channel_id=1, source_target_pairs={{0,96},{16,112},{32,64},{48,80},{64,32},{80,48},{96,0},{112,16},{1... | collective-permute-start | bytes 786440 | tf_op jit(solution)/shard_map/ppermute | solution.py:220
  30.0 3.3 %collective-permute-done.2.refs_1_ = bf16[8,128,256]{2,1,0:T(8,128)(2,1)S(1)} collective-permute-done((bf16[8,128,256]{2,1,0:T(8,128)(2,1)S(1)}, bf16[8,128,256]{2,1,0:T(8,128)(2,1)S(1)}, u32[]{:S(2)}, u32[]{:S(2)}) %collective-permute-start.2) | collective-permute-done | bytes 524320 | tf_op jit(solution)/shard_map/ppermute | solution.py:220
  33.3 0.5 shard_map.43
  33.8 3.2 %collective-permute-start.6 = (bf16[4,128,256]{2,1,0:T(8,128)(2,1)S(1)}, bf16[4,128,256]{2,1,0:T(8,128)(2,1)S(1)}, u32[]{:S(2)}, u32[]{:S(2)}) collective-permute-start(bf16[4,128,256]{2,1,0:T(8,128)(2,1)S(1)} %get-tuple-element.40.refs_0_), channel_id=1, source_target_pairs={{0,2},{1,3},{2,0},{3,1},{4,6},{5,7},{6,4},{7,5},{8,10},{9,11},{10,... | collective-permute-start | bytes 786440 | tf_op jit(solution)/shard_map/ppermute | solution.py:220
  37.0 4.2 %collective-permute-done.7.refs_1_ = bf16[4,128,256]{2,1,0:T(8,128)(2,1)S(1)} collective-permute-done((bf16[4,128,256]{2,1,0:T(8,128)(2,1)S(1)}, bf16[4,128,256]{2,1,0:T(8,128)(2,1)S(1)}, u32[]{:S(2)}, u32[]{:S(2)}) %collective-permute-start.7) | collective-permute-done | bytes 262176 | tf_op jit(solution)/shard_map/ppermute | solution.py:220
  41.2 0.4 shard_map.44
  41.6 1.7 %collective-permute-start.9 = (bf16[2,128,256]{2,1,0:T(8,128)(2,1)S(1)}, bf16[2,128,256]{2,1,0:T(8,128)(2,1)S(1)}, u32[]{:S(2)}, u32[]{:S(2)}) collective-permute-start(bf16[2,128,256]{2,1,0:T(8,128)(2,1)S(1)} %get-tuple-element.44), channel_id=1, source_target_pairs={{0,32},{16,48},{32,0},{48,16},{64,96},{80,112},{96,64},{112,80},{1... | collective-permute-start | bytes 393224 | tf_op jit(solution)/shard_map/ppermute | solution.py:220
  43.2 0.8 collective-permute-start.5
  44.1 2.6 %collective-permute-done.9.refs_1_ = bf16[2,128,256]{2,1,0:T(8,128)(2,1)S(1)} collective-permute-done((bf16[2,128,256]{2,1,0:T(8,128)(2,1)S(1)}, bf16[2,128,256]{2,1,0:T(8,128)(2,1)S(1)}, u32[]{:S(2)}, u32[]{:S(2)}) %collective-permute-start.9) | collective-permute-done | bytes 131104 | tf_op jit(solution)/shard_map/ppermute | solution.py:220
  46.6 0.4 shard_map.45.refs_3_.refs_0_
  47.0 2.0 %collective-permute-start.13 = (bf16[4,128,256]{2,1,0:T(8,128)(2,1)S(1)}, bf16[4,128,256]{2,1,0:T(8,128)(2,1)S(1)}, u32[]{:S(2)}, u32[]{:S(2)}) collective-permute-start(bf16[4,128,256]{2,1,0:T(8,128)(2,1)S(1)} %shard_map.45.refs_3_.refs_0_), channel_id=1, source_target_pairs={{0,4},{1,5},{2,6},{3,7},{4,0},{5,1},{6,2},{7,3},{8,12},{9,13},{10,... | collective-permute-start | bytes 786440 | tf_op jit(solution)/shard_map/ppermute | solution.py:220
  49.0 0.4 shard_map.46
  49.4 1.6 %collective-permute-start.14 = (bf16[2,128,256]{2,1,0:T(8,128)(2,1)S(1)}, bf16[2,128,256]{2,1,0:T(8,128)(2,1)S(1)}, u32[]{:S(2)}, u32[]{:S(2)}) collective-permute-start(bf16[2,128,256]{2,1,0:T(8,128)(2,1)S(1)} %get-tuple-element.49), channel_id=1, source_target_pairs={{0,32},{16,48},{32,0},{48,16},{64,96},{80,112},{96,64},{112,80},{1... | collective-permute-start | bytes 393224 | tf_op jit(solution)/shard_map/ppermute | solution.py:220
  51.0 0.8 collective-permute-start.4
  51.9 0.4 shard_map.47
  52.2 1.9 %collective-permute-start.12 = (bf16[2,128,256]{2,1,0:T(8,128)(2,1)S(1)}, bf16[2,128,256]{2,1,0:T(8,128)(2,1)S(1)}, u32[]{:S(2)}, u32[]{:S(2)}) collective-permute-start(bf16[2,128,256]{2,1,0:T(8,128)(2,1)S(1)} %get-tuple-element.48), channel_id=1, source_target_pairs={{0,32},{16,48},{32,0},{48,16},{64,96},{80,112},{96,64},{112,80},{1... | collective-permute-start | bytes 393224 | tf_op jit(solution)/shard_map/ppermute | solution.py:220
  54.2 1.4 %collective-permute-done.14.refs_1_ = bf16[2,128,256]{2,1,0:T(8,128)(2,1)S(1)} collective-permute-done((bf16[2,128,256]{2,1,0:T(8,128)(2,1)S(1)}, bf16[2,128,256]{2,1,0:T(8,128)(2,1)S(1)}, u32[]{:S(2)}, u32[]{:S(2)}) %collective-permute-start.14) | collective-permute-done | bytes 131104 | tf_op jit(solution)/shard_map/ppermute | solution.py:220
  55.6 0.4 shard_map.48.refs_4_.refs_0_
  55.9 1.3 %collective-permute-start.16 = (bf16[4,128,256]{2,1,0:T(8,128)(2,1)S(1)}, bf16[4,128,256]{2,1,0:T(8,128)(2,1)S(1)}, u32[]{:S(2)}, u32[]{:S(2)}) collective-permute-start(bf16[4,128,256]{2,1,0:T(8,128)(2,1)S(1)} %shard_map.48.refs_4_.refs_0_), channel_id=1, source_target_pairs={{0,4},{1,5},{2,6},{3,7},{4,0},{5,1},{6,2},{7,3},{8,12},{9,13},{10,... | collective-permute-start | bytes 786440 | tf_op jit(solution)/shard_map/ppermute | solution.py:220
  57.3 0.4 shard_map.49
  57.7 3.0 %collective-permute-start.17 = (bf16[2,128,256]{2,1,0:T(8,128)(2,1)S(1)}, bf16[2,128,256]{2,1,0:T(8,128)(2,1)S(1)}, u32[]{:S(2)}, u32[]{:S(2)}) collective-permute-start(bf16[2,128,256]{2,1,0:T(8,128)(2,1)S(1)} %get-tuple-element.53), channel_id=1, source_target_pairs={{0,64},{16,80},{32,96},{48,112},{64,0},{80,16},{96,32},{112,48},{1... | collective-permute-start | bytes 393224 | tf_op jit(solution)/shard_map/ppermute | solution.py:220
  60.6 0.4 shard_map.50.refs_3_.refs_0_
  61.0 1.2 %collective-permute-start.19 = (bf16[4,128,256]{2,1,0:T(8,128)(2,1)S(1)}, bf16[4,128,256]{2,1,0:T(8,128)(2,1)S(1)}, u32[]{:S(2)}, u32[]{:S(2)}) collective-permute-start(bf16[4,128,256]{2,1,0:T(8,128)(2,1)S(1)} %shard_map.50.refs_3_.refs_0_), channel_id=1, source_target_pairs={{0,4},{1,5},{2,6},{3,7},{4,0},{5,1},{6,2},{7,3},{8,12},{9,13},{10,... | collective-permute-start | bytes 786440 | tf_op jit(solution)/shard_map/ppermute | solution.py:220
  62.2 0.4 shard_map.51
  62.6 1.5 %collective-permute-start.15 = (bf16[2,128,256]{2,1,0:T(8,128)(2,1)S(1)}, bf16[2,128,256]{2,1,0:T(8,128)(2,1)S(1)}, u32[]{:S(2)}, u32[]{:S(2)}) collective-permute-start(bf16[2,128,256]{2,1,0:T(8,128)(2,1)S(1)} %get-tuple-element.52), channel_id=1, source_target_pairs={{0,32},{16,48},{32,0},{48,16},{64,96},{80,112},{96,64},{112,80},{1... | collective-permute-start | bytes 393224 | tf_op jit(solution)/shard_map/ppermute | solution.py:220
  64.1 1.1 %collective-permute-done.17.refs_1_ = bf16[2,128,256]{2,1,0:T(8,128)(2,1)S(1)} collective-permute-done((bf16[2,128,256]{2,1,0:T(8,128)(2,1)S(1)}, bf16[2,128,256]{2,1,0:T(8,128)(2,1)S(1)}, u32[]{:S(2)}, u32[]{:S(2)}) %collective-permute-start.17) | collective-permute-done | bytes 131104 | tf_op jit(solution)/shard_map/ppermute | solution.py:220
  65.2 0.4 shard_map.52.refs_4_.refs_0_
  65.6 0.4 shard_map.53
  66.0 2.1 %collective-permute-start.21 = (bf16[2,128,256]{2,1,0:T(8,128)(2,1)S(1)}, bf16[2,128,256]{2,1,0:T(8,128)(2,1)S(1)}, u32[]{:S(2)}, u32[]{:S(2)}) collective-permute-start(bf16[2,128,256]{2,1,0:T(8,128)(2,1)S(1)} %get-tuple-element.58), channel_id=1, source_target_pairs={{0,64},{16,80},{32,96},{48,112},{64,0},{80,16},{96,32},{112,48},{1... | collective-permute-start | bytes 393224 | tf_op jit(solution)/shard_map/ppermute | solution.py:220
  68.1 0.4 shard_map.54.refs_4_.refs_0_
  68.5 1.2 %collective-permute-start.18 = (bf16[4,128,256]{2,1,0:T(8,128)(2,1)S(1)}, bf16[4,128,256]{2,1,0:T(8,128)(2,1)S(1)}, u32[]{:S(2)}, u32[]{:S(2)}) collective-permute-start(bf16[4,128,256]{2,1,0:T(8,128)(2,1)S(1)} %shard_map.54.refs_4_.refs_0_), channel_id=1, source_target_pairs={{0,4},{1,5},{2,6},{3,7},{4,0},{5,1},{6,2},{7,3},{8,12},{9,13},{10,... | collective-permute-start | bytes 786440 | tf_op jit(solution)/shard_map/ppermute | solution.py:220
  69.7 3.7 %collective-permute-start.24 = (bf16[4,128,256]{2,1,0:T(8,128)(2,1)S(1)}, bf16[4,128,256]{2,1,0:T(8,128)(2,1)S(1)}, u32[]{:S(2)}, u32[]{:S(2)}) collective-permute-start(bf16[4,128,256]{2,1,0:T(8,128)(2,1)S(1)} %shard_map.52.refs_4_.refs_0_), channel_id=1, source_target_pairs={{0,8},{1,9},{2,10},{3,11},{4,12},{5,13},{6,14},{7,15},{8,0},{9,1},... | collective-permute-start | bytes 786440 | tf_op jit(solution)/shard_map/ppermute | solution.py:220
  73.4 0.4 shard_map.55
  73.8 1.2 %collective-permute-start.20 = (bf16[2,128,256]{2,1,0:T(8,128)(2,1)S(1)}, bf16[2,128,256]{2,1,0:T(8,128)(2,1)S(1)}, u32[]{:S(2)}, u32[]{:S(2)}) collective-permute-start(bf16[2,128,256]{2,1,0:T(8,128)(2,1)S(1)} %get-tuple-element.57), channel_id=1, source_target_pairs={{0,64},{16,80},{32,96},{48,112},{64,0},{80,16},{96,32},{112,48},{1... | collective-permute-start | bytes 393224 | tf_op jit(solution)/shard_map/ppermute | solution.py:220
  75.0 0.4 shard_map.56.refs_6_.refs_0_
  75.4 1.4 %collective-permute-start.23 = (bf16[4,128,256]{2,1,0:T(8,128)(2,1)S(1)}, bf16[4,128,256]{2,1,0:T(8,128)(2,1)S(1)}, u32[]{:S(2)}, u32[]{:S(2)}) collective-permute-start(bf16[4,128,256]{2,1,0:T(8,128)(2,1)S(1)} %shard_map.56.refs_6_.refs_0_), channel_id=1, source_target_pairs={{0,8},{1,9},{2,10},{3,11},{4,12},{5,13},{6,14},{7,15},{8,0},{9,1},... | collective-permute-start | bytes 786440 | tf_op jit(solution)/shard_map/ppermute | solution.py:220
  76.8 4.4 %collective-permute-done.20.refs_1_ = bf16[2,128,256]{2,1,0:T(8,128)(2,1)S(1)} collective-permute-done((bf16[2,128,256]{2,1,0:T(8,128)(2,1)S(1)}, bf16[2,128,256]{2,1,0:T(8,128)(2,1)S(1)}, u32[]{:S(2)}, u32[]{:S(2)}) %collective-permute-start.20) | collective-permute-done | bytes 131104 | tf_op jit(solution)/shard_map/ppermute | solution.py:220
  81.6 0.4 shard_map.58
  82.0 1.1 %collective-permute-start.22 = (bf16[2,128,256]{2,1,0:T(8,128)(2,1)S(1)}, bf16[2,128,256]{2,1,0:T(8,128)(2,1)S(1)}, u32[]{:S(2)}, u32[]{:S(2)}) collective-permute-start(bf16[2,128,256]{2,1,0:T(8,128)(2,1)S(1)} %get-tuple-element.60), channel_id=1, source_target_pairs={{0,64},{16,80},{32,96},{48,112},{64,0},{80,16},{96,32},{112,48},{1... | collective-permute-start | bytes 393224 | tf_op jit(solution)/shard_map/ppermute | solution.py:220
  83.1 2.0 %collective-permute-start.26 = (bf16[4,128,256]{2,1,0:T(8,128)(2,1)S(1)}, bf16[4,128,256]{2,1,0:T(8,128)(2,1)S(1)}, u32[]{:S(2)}, u32[]{:S(2)}) collective-permute-start(bf16[4,128,256]{2,1,0:T(8,128)(2,1)S(1)} %shard_map.57.refs_4_.refs_0_), channel_id=1, source_target_pairs={{0,8},{1,9},{2,10},{3,11},{4,12},{5,13},{6,14},{7,15},{8,0},{9,1},... | collective-permute-start | bytes 786440 | tf_op jit(solution)/shard_map/ppermute | solution.py:220
  85.1 1.2 %collective-permute-done.24.refs_1_ = bf16[4,128,256]{2,1,0:T(8,128)(2,1)S(1)} collective-permute-done((bf16[4,128,256]{2,1,0:T(8,128)(2,1)S(1)}, bf16[4,128,256]{2,1,0:T(8,128)(2,1)S(1)}, u32[]{:S(2)}, u32[]{:S(2)}) %collective-permute-start.24) | collective-permute-done | bytes 262176 | tf_op jit(solution)/shard_map/ppermute | solution.py:220
  86.2 0.4 shard_map.59.refs_6_
  86.9 4.9 %collective-permute-done.23.refs_1_ = bf16[4,128,256]{2,1,0:T(8,128)(2,1)S(1)} collective-permute-done((bf16[4,128,256]{2,1,0:T(8,128)(2,1)S(1)}, bf16[4,128,256]{2,1,0:T(8,128)(2,1)S(1)}, u32[]{:S(2)}, u32[]{:S(2)}) %collective-permute-start.23) | collective-permute-done | bytes 262176 | tf_op jit(solution)/shard_map/ppermute | solution.py:220
  91.8 0.4 shard_map.60.refs_6_
  92.2 0.4 shard_map.61.refs_6_.refs_0_
  93.0 2.8 %collective-permute-done.26.refs_1_ = bf16[4,128,256]{2,1,0:T(8,128)(2,1)S(1)} collective-permute-done((bf16[4,128,256]{2,1,0:T(8,128)(2,1)S(1)}, bf16[4,128,256]{2,1,0:T(8,128)(2,1)S(1)}, u32[]{:S(2)}, u32[]{:S(2)}) %collective-permute-start.26) | collective-permute-done | bytes 262176 | tf_op jit(solution)/shard_map/ppermute | solution.py:220
  95.9 0.4 shard_map.62.refs_6_.k._
  96.2 1.4 %shard_map.64._ = bf16[2,1024,256]{2,1,0:T(8,128)(2,1)} custom-call(bf16[2,8,1024,128]{3,2,1,0:T(8,128)(2,1)S(1)} %bitcast.4, bf16[4,128,256]{2,1,0:T(8,128)(2,1)S(1)} %shard_map.62.refs_6_.k._, bf16[4,128,256]{2,1,0:T(8,128)(2,1)S(1)} %collective-permute-done.28.c, bf16[4,128,256]{2,1,0:T(8,128)(2,1)S(1)} %shard_map.62.refs_6_.k._), custom_call_target="tpu_custom_call" | custom-call | flops 536870912 | bytes 2621440 | tf_op jit(solution)/shard_map/pallas_call | solution.py:199
  97.7 2.9 %collective-permute-done.25.refs_1_ = bf16[4,128,256]{2,1,0:T(8,128)(2,1)S(1)} collective-permute-done((bf16[4,128,256]{2,1,0:T(8,128)(2,1)S(1)}, bf16[4,128,256]{2,1,0:T(8,128)(2,1)S(1)}, u32[]{:S(2)}, u32[]{:S(2)}) %collective-permute-start.25) | collective-permute-done | bytes 262176 | tf_op jit(solution)/shard_map/ppermute | solution.py:220
  100.5 0.4 shard_map.63.k
  100.9 1.4 %shard_map.65 = bf16[2,1024,256]{2,1,0:T(8,128)(2,1)} custom-call(bf16[2,8,1024,128]{3,2,1,0:T(8,128)(2,1)S(1)} %bitcast.5, bf16[4,128,256]{2,1,0:T(8,128)(2,1)S(1)} %shard_map.63.k, bf16[4,128,256]{2,1,0:T(8,128)(2,1)S(1)} %collective-permute-done.27.c, bf16[2,1024,256]{2,1,0:T(8,128)(2,1)} %shard_map.64._), custom_call_target="tpu_custom_call", output_to_operand_aliasing={{}: (3, {})} | custom-call | flops 536870912 | bytes 2621440 | tf_op jit(solution)/shard_map/pallas_call | solution.py:199
  (25 shorter events, 1.5 us)
Async XLA Ops:
  4.7 2.0 %collective-permute-start.1 = (bf16[8,128,256]{2,1,0:T(8,128)(2,1)S(1)}, bf16[8,128,256]{2,1,0:T(8,128)(2,1)S(1)}, u32[]{:S(2)}, u32[]{:S(2)}) collective-permute-start(bf16[8,128,256]{2,1,0:T(8,128)(2,1)S(1)} %get-tuple-element.35._.refs_0_), channel_id=1, source_target_pairs={{0,1},{1,0},{2,3},{3,2},{4,5},{5,4},{6,7},{7,6},{8,9},{9,8},{10,11... | collective-permute-start | bytes 1572872 | tf_op jit(solution)/shard_map/ppermute | solution.py:220
  4.8 4.1 %collective-permute-start = (bf16[8,128,256]{2,1,0:T(8,128)(2,1)S(1)}, bf16[8,128,256]{2,1,0:T(8,128)(2,1)S(1)}, u32[]{:S(2)}, u32[]{:S(2)}) collective-permute-start(bf16[8,128,256]{2,1,0:T(8,128)(2,1)S(1)} %get-tuple-element.33.refs_0_), channel_id=1, source_target_pairs={{0,1},{1,0},{2,3},{3,2},{4,5},{5,4},{6,7},{7,6},{8,9},{9,8},{10,11... | collective-permute-start | bytes 1572872 | tf_op jit(solution)/shard_map/ppermute | solution.py:220
  7.2 14.8 %collective-permute-start.3 = (bf16[8,128,256]{2,1,0:T(8,128)(2,1)S(1)}, bf16[8,128,256]{2,1,0:T(8,128)(2,1)S(1)}, u32[]{:S(2)}, u32[]{:S(2)}) collective-permute-start(bf16[8,128,256]{2,1,0:T(8,128)(2,1)S(1)} %shard_map.39.refs_3_.refs_0_), channel_id=1, source_target_pairs={{0,16},{16,0},{32,48},{48,32},{64,80},{80,64},{96,112},{112,96},{1... | collective-permute-start | bytes 1572872 | tf_op jit(solution)/shard_map/ppermute | solution.py:220
  11.0 30.2 %collective-permute-start.8 = (bf16[12,2,64,256]{3,2,1,0:T(8,128)(2,1)S(1)}, bf16[12,2,64,256]{3,2,1,0:T(8,128)(2,1)S(1)}, u32[]{:S(2)}, u32[]{:S(2)}) collective-permute-start(bf16[12,2,64,256]{3,2,1,0:T(8,128)(2,1)S(1)} %get-tuple-element.42), channel_id=1, source_target_pairs={{0,32},{16,48},{32,0},{48,16},{64,96},{80,112},{96,64},{112,80},{1... | collective-permute-start | bytes 2359304 | tf_op jit(solution)/shard_map/ppermute | solution.py:220
  12.7 20.6 %collective-permute-start.2 = (bf16[8,128,256]{2,1,0:T(8,128)(2,1)S(1)}, bf16[8,128,256]{2,1,0:T(8,128)(2,1)S(1)}, u32[]{:S(2)}, u32[]{:S(2)}) collective-permute-start(bf16[8,128,256]{2,1,0:T(8,128)(2,1)S(1)} %shard_map.40._.refs_0_), channel_id=1, source_target_pairs={{0,16},{16,0},{32,48},{48,32},{64,80},{80,64},{96,112},{112,96},{1... | collective-permute-start | bytes 1572872 | tf_op jit(solution)/shard_map/ppermute | solution.py:220
  22.6 18.6 %collective-permute-start.7 = (bf16[4,128,256]{2,1,0:T(8,128)(2,1)S(1)}, bf16[4,128,256]{2,1,0:T(8,128)(2,1)S(1)}, u32[]{:S(2)}, u32[]{:S(2)}) collective-permute-start(bf16[4,128,256]{2,1,0:T(8,128)(2,1)S(1)} %get-tuple-element.41.refs_0_), channel_id=1, source_target_pairs={{0,2},{1,3},{2,0},{3,1},{4,6},{5,7},{6,4},{7,5},{8,10},{9,11},{10,... | collective-permute-start | bytes 786440 | tf_op jit(solution)/shard_map/ppermute | solution.py:220
  25.8 18.3 %collective-permute-start.10 = (bf16[4,2,64,256]{3,2,1,0:T(8,128)(2,1)S(1)}, bf16[4,2,64,256]{3,2,1,0:T(8,128)(2,1)S(1)}, u32[]{:S(2)}, u32[]{:S(2)}) collective-permute-start(bf16[4,2,64,256]{3,2,1,0:T(8,128)(2,1)S(1)} %get-tuple-element.36.refs_3_), channel_id=1, source_target_pairs={{0,64},{16,80},{32,96},{48,112},{64,0},{80,16},{96,32},{112,48},{1... | collective-permute-start | bytes 786440 | tf_op jit(solution)/shard_map/ppermute | solution.py:220
  29.0 15.1 %collective-permute-start.11 = (bf16[4,2,64,256]{3,2,1,0:T(8,128)(2,1)S(1)}, bf16[4,2,64,256]{3,2,1,0:T(8,128)(2,1)S(1)}, u32[]{:S(2)}, u32[]{:S(2)}) collective-permute-start(bf16[4,2,64,256]{3,2,1,0:T(8,128)(2,1)S(1)} %get-tuple-element.45), channel_id=1, source_target_pairs={{0,96},{16,112},{32,64},{48,80},{64,32},{80,48},{96,0},{112,16},{1... | collective-permute-start | bytes 786440 | tf_op jit(solution)/shard_map/ppermute | solution.py:220
  33.8 15.2 %collective-permute-start.6 = (bf16[4,128,256]{2,1,0:T(8,128)(2,1)S(1)}, bf16[4,128,256]{2,1,0:T(8,128)(2,1)S(1)}, u32[]{:S(2)}, u32[]{:S(2)}) collective-permute-start(bf16[4,128,256]{2,1,0:T(8,128)(2,1)S(1)} %get-tuple-element.40.refs_0_), channel_id=1, source_target_pairs={{0,2},{1,3},{2,0},{3,1},{4,6},{5,7},{6,4},{7,5},{8,10},{9,11},{10,... | collective-permute-start | bytes 786440 | tf_op jit(solution)/shard_map/ppermute | solution.py:220
  41.6 5.0 %collective-permute-start.9 = (bf16[2,128,256]{2,1,0:T(8,128)(2,1)S(1)}, bf16[2,128,256]{2,1,0:T(8,128)(2,1)S(1)}, u32[]{:S(2)}, u32[]{:S(2)}) collective-permute-start(bf16[2,128,256]{2,1,0:T(8,128)(2,1)S(1)} %get-tuple-element.44), channel_id=1, source_target_pairs={{0,32},{16,48},{32,0},{48,16},{64,96},{80,112},{96,64},{112,80},{1... | collective-permute-start | bytes 393224 | tf_op jit(solution)/shard_map/ppermute | solution.py:220
  43.2 8.6 %collective-permute-start.5 = (bf16[4,128,256]{2,1,0:T(8,128)(2,1)S(1)}, bf16[4,128,256]{2,1,0:T(8,128)(2,1)S(1)}, u32[]{:S(2)}, u32[]{:S(2)}) collective-permute-start(bf16[4,128,256]{2,1,0:T(8,128)(2,1)S(1)} %get-tuple-element.38.refs_3_.refs_0_), channel_id=1, source_target_pairs={{0,2},{1,3},{2,0},{3,1},{4,6},{5,7},{6,4},{7,5},{8,10},{9,11},{10,... | collective-permute-start | bytes 786440 | tf_op jit(solution)/shard_map/ppermute | solution.py:220
  47.0 10.3 %collective-permute-start.13 = (bf16[4,128,256]{2,1,0:T(8,128)(2,1)S(1)}, bf16[4,128,256]{2,1,0:T(8,128)(2,1)S(1)}, u32[]{:S(2)}, u32[]{:S(2)}) collective-permute-start(bf16[4,128,256]{2,1,0:T(8,128)(2,1)S(1)} %shard_map.45.refs_3_.refs_0_), channel_id=1, source_target_pairs={{0,4},{1,5},{2,6},{3,7},{4,0},{5,1},{6,2},{7,3},{8,12},{9,13},{10,... | collective-permute-start | bytes 786440 | tf_op jit(solution)/shard_map/ppermute | solution.py:220
  49.4 6.2 %collective-permute-start.14 = (bf16[2,128,256]{2,1,0:T(8,128)(2,1)S(1)}, bf16[2,128,256]{2,1,0:T(8,128)(2,1)S(1)}, u32[]{:S(2)}, u32[]{:S(2)}) collective-permute-start(bf16[2,128,256]{2,1,0:T(8,128)(2,1)S(1)} %get-tuple-element.49), channel_id=1, source_target_pairs={{0,32},{16,48},{32,0},{48,16},{64,96},{80,112},{96,64},{112,80},{1... | collective-permute-start | bytes 393224 | tf_op jit(solution)/shard_map/ppermute | solution.py:220
  51.0 11.2 %collective-permute-start.4 = (bf16[4,128,256]{2,1,0:T(8,128)(2,1)S(1)}, bf16[4,128,256]{2,1,0:T(8,128)(2,1)S(1)}, u32[]{:S(2)}, u32[]{:S(2)}) collective-permute-start(bf16[4,128,256]{2,1,0:T(8,128)(2,1)S(1)} %get-tuple-element.39.refs_4_.refs_0_), channel_id=1, source_target_pairs={{0,2},{1,3},{2,0},{3,1},{4,6},{5,7},{6,4},{7,5},{8,10},{9,11},{10,... | collective-permute-start | bytes 786440 | tf_op jit(solution)/shard_map/ppermute | solution.py:220
  52.2 8.4 %collective-permute-start.12 = (bf16[2,128,256]{2,1,0:T(8,128)(2,1)S(1)}, bf16[2,128,256]{2,1,0:T(8,128)(2,1)S(1)}, u32[]{:S(2)}, u32[]{:S(2)}) collective-permute-start(bf16[2,128,256]{2,1,0:T(8,128)(2,1)S(1)} %get-tuple-element.48), channel_id=1, source_target_pairs={{0,32},{16,48},{32,0},{48,16},{64,96},{80,112},{96,64},{112,80},{1... | collective-permute-start | bytes 393224 | tf_op jit(solution)/shard_map/ppermute | solution.py:220
  55.9 9.6 %collective-permute-start.16 = (bf16[4,128,256]{2,1,0:T(8,128)(2,1)S(1)}, bf16[4,128,256]{2,1,0:T(8,128)(2,1)S(1)}, u32[]{:S(2)}, u32[]{:S(2)}) collective-permute-start(bf16[4,128,256]{2,1,0:T(8,128)(2,1)S(1)} %shard_map.48.refs_4_.refs_0_), channel_id=1, source_target_pairs={{0,4},{1,5},{2,6},{3,7},{4,0},{5,1},{6,2},{7,3},{8,12},{9,13},{10,... | collective-permute-start | bytes 786440 | tf_op jit(solution)/shard_map/ppermute | solution.py:220
  57.7 7.5 %collective-permute-start.17 = (bf16[2,128,256]{2,1,0:T(8,128)(2,1)S(1)}, bf16[2,128,256]{2,1,0:T(8,128)(2,1)S(1)}, u32[]{:S(2)}, u32[]{:S(2)}) collective-permute-start(bf16[2,128,256]{2,1,0:T(8,128)(2,1)S(1)} %get-tuple-element.53), channel_id=1, source_target_pairs={{0,64},{16,80},{32,96},{48,112},{64,0},{80,16},{96,32},{112,48},{1... | collective-permute-start | bytes 393224 | tf_op jit(solution)/shard_map/ppermute | solution.py:220
  61.0 12.4 %collective-permute-start.19 = (bf16[4,128,256]{2,1,0:T(8,128)(2,1)S(1)}, bf16[4,128,256]{2,1,0:T(8,128)(2,1)S(1)}, u32[]{:S(2)}, u32[]{:S(2)}) collective-permute-start(bf16[4,128,256]{2,1,0:T(8,128)(2,1)S(1)} %shard_map.50.refs_3_.refs_0_), channel_id=1, source_target_pairs={{0,4},{1,5},{2,6},{3,7},{4,0},{5,1},{6,2},{7,3},{8,12},{9,13},{10,... | collective-permute-start | bytes 786440 | tf_op jit(solution)/shard_map/ppermute | solution.py:220
  62.6 5.5 %collective-permute-start.15 = (bf16[2,128,256]{2,1,0:T(8,128)(2,1)S(1)}, bf16[2,128,256]{2,1,0:T(8,128)(2,1)S(1)}, u32[]{:S(2)}, u32[]{:S(2)}) collective-permute-start(bf16[2,128,256]{2,1,0:T(8,128)(2,1)S(1)} %get-tuple-element.52), channel_id=1, source_target_pairs={{0,32},{16,48},{32,0},{48,16},{64,96},{80,112},{96,64},{112,80},{1... | collective-permute-start | bytes 393224 | tf_op jit(solution)/shard_map/ppermute | solution.py:220
  66.0 9.1 %collective-permute-start.21 = (bf16[2,128,256]{2,1,0:T(8,128)(2,1)S(1)}, bf16[2,128,256]{2,1,0:T(8,128)(2,1)S(1)}, u32[]{:S(2)}, u32[]{:S(2)}) collective-permute-start(bf16[2,128,256]{2,1,0:T(8,128)(2,1)S(1)} %get-tuple-element.58), channel_id=1, source_target_pairs={{0,64},{16,80},{32,96},{48,112},{64,0},{80,16},{96,32},{112,48},{1... | collective-permute-start | bytes 393224 | tf_op jit(solution)/shard_map/ppermute | solution.py:220
  68.5 13.2 %collective-permute-start.18 = (bf16[4,128,256]{2,1,0:T(8,128)(2,1)S(1)}, bf16[4,128,256]{2,1,0:T(8,128)(2,1)S(1)}, u32[]{:S(2)}, u32[]{:S(2)}) collective-permute-start(bf16[4,128,256]{2,1,0:T(8,128)(2,1)S(1)} %shard_map.54.refs_4_.refs_0_), channel_id=1, source_target_pairs={{0,4},{1,5},{2,6},{3,7},{4,0},{5,1},{6,2},{7,3},{8,12},{9,13},{10,... | collective-permute-start | bytes 786440 | tf_op jit(solution)/shard_map/ppermute | solution.py:220
  69.7 16.5 %collective-permute-start.24 = (bf16[4,128,256]{2,1,0:T(8,128)(2,1)S(1)}, bf16[4,128,256]{2,1,0:T(8,128)(2,1)S(1)}, u32[]{:S(2)}, u32[]{:S(2)}) collective-permute-start(bf16[4,128,256]{2,1,0:T(8,128)(2,1)S(1)} %shard_map.52.refs_4_.refs_0_), channel_id=1, source_target_pairs={{0,8},{1,9},{2,10},{3,11},{4,12},{5,13},{6,14},{7,15},{8,0},{9,1},... | collective-permute-start | bytes 786440 | tf_op jit(solution)/shard_map/ppermute | solution.py:220
  73.8 7.5 %collective-permute-start.20 = (bf16[2,128,256]{2,1,0:T(8,128)(2,1)S(1)}, bf16[2,128,256]{2,1,0:T(8,128)(2,1)S(1)}, u32[]{:S(2)}, u32[]{:S(2)}) collective-permute-start(bf16[2,128,256]{2,1,0:T(8,128)(2,1)S(1)} %get-tuple-element.57), channel_id=1, source_target_pairs={{0,64},{16,80},{32,96},{48,112},{64,0},{80,16},{96,32},{112,48},{1... | collective-permute-start | bytes 393224 | tf_op jit(solution)/shard_map/ppermute | solution.py:220
  75.4 16.5 %collective-permute-start.23 = (bf16[4,128,256]{2,1,0:T(8,128)(2,1)S(1)}, bf16[4,128,256]{2,1,0:T(8,128)(2,1)S(1)}, u32[]{:S(2)}, u32[]{:S(2)}) collective-permute-start(bf16[4,128,256]{2,1,0:T(8,128)(2,1)S(1)} %shard_map.56.refs_6_.refs_0_), channel_id=1, source_target_pairs={{0,8},{1,9},{2,10},{3,11},{4,12},{5,13},{6,14},{7,15},{8,0},{9,1},... | collective-permute-start | bytes 786440 | tf_op jit(solution)/shard_map/ppermute | solution.py:220
  82.0 10.2 %collective-permute-start.22 = (bf16[2,128,256]{2,1,0:T(8,128)(2,1)S(1)}, bf16[2,128,256]{2,1,0:T(8,128)(2,1)S(1)}, u32[]{:S(2)}, u32[]{:S(2)}) collective-permute-start(bf16[2,128,256]{2,1,0:T(8,128)(2,1)S(1)} %get-tuple-element.60), channel_id=1, source_target_pairs={{0,64},{16,80},{32,96},{48,112},{64,0},{80,16},{96,32},{112,48},{1... | collective-permute-start | bytes 393224 | tf_op jit(solution)/shard_map/ppermute | solution.py:220
  83.1 12.7 %collective-permute-start.26 = (bf16[4,128,256]{2,1,0:T(8,128)(2,1)S(1)}, bf16[4,128,256]{2,1,0:T(8,128)(2,1)S(1)}, u32[]{:S(2)}, u32[]{:S(2)}) collective-permute-start(bf16[4,128,256]{2,1,0:T(8,128)(2,1)S(1)} %shard_map.57.refs_4_.refs_0_), channel_id=1, source_target_pairs={{0,8},{1,9},{2,10},{3,11},{4,12},{5,13},{6,14},{7,15},{8,0},{9,1},... | collective-permute-start | bytes 786440 | tf_op jit(solution)/shard_map/ppermute | solution.py:220
  86.6 9.6 %copy-start = (bf16[1,2,8,1024,128]{4,3,2,1,0:T(8,128)(2,1)S(1)}, bf16[1,2,8,1024,128]{4,3,2,1,0:T(8,128)(2,1)}, u32[]{:S(2)}) copy-start(bf16[1,2,8,1024,128]{4,3,2,1,0:T(8,128)(2,1)} %param.5) | copy-start | bytes 12582916
  86.6 9.6 %collective-permute-start.28 = (bf16[4,128,256]{2,1,0:T(8,128)(2,1)S(1)}, bf16[4,128,256]{2,1,0:T(8,128)(2,1)S(1)}, u32[]{:S(2)}, u32[]{:S(2)}) collective-permute-start(bf16[4,128,256]{2,1,0:T(8,128)(2,1)S(1)} %shard_map.59.refs_6_), channel_id=1, source_target_pairs={{0,16},{16,0},{32,48},{48,32},{64,80},{80,64},{96,112},{112,96},{1... | collective-permute-start | bytes 786440 | tf_op jit(solution)/shard_map/ppermute | solution.py:220
  92.6 8.0 %collective-permute-start.25 = (bf16[4,128,256]{2,1,0:T(8,128)(2,1)S(1)}, bf16[4,128,256]{2,1,0:T(8,128)(2,1)S(1)}, u32[]{:S(2)}, u32[]{:S(2)}) collective-permute-start(bf16[4,128,256]{2,1,0:T(8,128)(2,1)S(1)} %shard_map.61.refs_6_.refs_0_), channel_id=1, source_target_pairs={{0,8},{1,9},{2,10},{3,11},{4,12},{5,13},{6,14},{7,15},{8,0},{9,1},... | collective-permute-start | bytes 786440 | tf_op jit(solution)/shard_map/ppermute | solution.py:220
  92.7 8.2 %collective-permute-start.27 = (bf16[4,128,256]{2,1,0:T(8,128)(2,1)S(1)}, bf16[4,128,256]{2,1,0:T(8,128)(2,1)S(1)}, u32[]{:S(2)}, u32[]{:S(2)}) collective-permute-start(bf16[4,128,256]{2,1,0:T(8,128)(2,1)S(1)} %shard_map.60.refs_6_), channel_id=1, source_target_pairs={{0,16},{16,0},{32,48},{48,32},{64,80},{80,64},{96,112},{112,96},{1... | collective-permute-start | bytes 786440 | tf_op jit(solution)/shard_map/ppermute | solution.py:220
